TPU v7x, 32 devices: a whole 2x2x4 slice. The times are simulated.
32 devices in a mesh: cores: 4 (over y, core), samp: 8 (over z, x).
Axes of the slice: x: 2, y: 2, z: 4, core: 2. Of those that a mesh axis runs over, the one named last changes fastest.
Arguments:
- cores: float32 [4, 512, 2304], P('cores'), may hold values from -0.875 to 0.875
- indices: int32 [8192, 4], P('samp'), may hold values from 0 to 511
- observed: float32 [8192], P('samp'), may hold values from -6 to 6
- step_size: float32 [], replicated, may hold values from 0.2 to 0.6
Outputs:
- new_cores: float32 [4, 512, 2304], P('cores', 'samp')
All inputs are finite; a program needn't handle non-finite values.
Results may differ from a plain program's by a relative error of at most 0.0003.
Values sent between devices are 32-bit elements; how exact they have to be, the bound alone decides.
A program may use at most 128 MiB of HBM per device.

v0:
```python
import functools

import jax
import jax.numpy as jnp
from jax import lax
from jax.experimental import pallas as pl
from jax.experimental.pallas import tpu as pltpu
from jax.sharding import PartitionSpec as P

R = 48
N = 512
W = 64

HIGH = lax.Precision.HIGHEST
MESH = pl.DeviceIdType.MESH
F32 = jnp.float32
BF16 = jnp.bfloat16


def split(x):
    high = x.astype(BF16)
    low = (x - high.astype(F32)).astype(BF16)
    return high, low


def three(x):
    high, low = split(x)
    return jnp.concatenate([high, low, high], axis=0)


def weigh(mat, ustack):
    high, low = split(mat)
    return jnp.dot(jnp.concatenate([high, high, low], axis=1), ustack, preferred_element_type=F32)


def tall_of(wide, pairs):
    return jnp.concatenate([wide[:, 128 * p:128 * p + 128] for p in range(pairs)], axis=0)


def gram_kernel(ncores, nsamp, pairs, uwide, hprev, hown, sendbuf, got_prev, got_own,
                send_own, send_next, recv_own, recv_prev):
    mine = lax.axis_index("cores")
    me = lax.axis_index("samp")
    barrier = pltpu.get_barrier_semaphore()
    has_prev = mine > 0
    has_next = mine < ncores - 1

    def greet(mode, other):
        pl.semaphore_signal(barrier, inc=1, device_id=(mode, other), device_id_type=MESH)

    for d in range(1, nsamp):
        greet(mine, lax.rem(me + d, nsamp))

    @pl.when(has_prev)
    def _():
        for d in range(nsamp):
            greet(mine - 1, lax.rem(me + d, nsamp))

    pl.semaphore_wait(barrier, nsamp - 1 + nsamp * jnp.minimum(ncores - 1 - mine, 1))

    def own_copy(d):
        return pltpu.make_async_remote_copy(
            src_ref=sendbuf, dst_ref=got_own.at[d - 1], send_sem=send_own.at[d - 1],
            recv_sem=recv_own.at[d - 1], device_id=(mine, lax.rem(me + d, nsamp)), device_id_type=MESH)

    def next_copy(d):
        return pltpu.make_async_remote_copy(
            src_ref=sendbuf, dst_ref=got_prev.at[d], send_sem=send_next.at[d],
            recv_sem=recv_prev.at[d], device_id=(mine + 1, lax.rem(me + d, nsamp)), device_id_type=MESH)

    ustack = three(uwide[...])
    uth, utl = split(tall_of(uwide[0:R, :], pairs).T)

    def unpack(x):
        return jnp.concatenate([x[:, :W], x[:, W:]], axis=0)

    row = lax.broadcasted_iota(jnp.int32, (R, W), 0)
    lane = lax.broadcasted_iota(jnp.int32, (R, W), 1)
    eye = (row == lane).astype(F32)
    hprev[...] = eye
    hown[...] = eye

    @pl.when(has_prev)
    def _():
        total = jnp.zeros((R // 2, 128), F32)
        for d in range(nsamp):
            pltpu.make_async_remote_copy(
                src_ref=sendbuf, dst_ref=got_prev.at[d], send_sem=send_next.at[d],
                recv_sem=recv_prev.at[d], device_id=(mine, me), device_id_type=MESH).wait_recv()
            total = total + got_prev[d]
        hprev[...] = unpack(total)

    @pl.when(has_next)
    def _():
        before = hprev[...]
        wh, wl = split(tall_of(weigh(before, ustack), pairs))
        both = jnp.dot(uth, wh, preferred_element_type=F32)
        both = both + jnp.dot(uth, wl, preferred_element_type=F32)
        both = both + jnp.dot(utl, wh, preferred_element_type=F32)
        gram = (both[:R, :W] + both[W:W + R, W:]) * (1.0 / N)
        sendbuf[...] = jnp.concatenate([gram[:R // 2], gram[R // 2:]], axis=1)
        for d in range(nsamp):
            next_copy(d).start()
        for d in range(1, nsamp):
            own_copy(d).start()
        total = sendbuf[...]
        for d in range(1, nsamp):
            own_copy(d).wait_recv()
            total = total + got_own[d - 1]
        hown[...] = unpack(total)
        for d in range(nsamp):
            next_copy(d).wait_send()
        for d in range(1, nsamp):
            own_copy(d).wait_send()


def picker(idx_ref):
    count = idx_ref.shape[1]
    row = lax.broadcasted_iota(jnp.int32, (N, count), 0)
    return jnp.where(row == idx_ref[...], 1.0, 0.0).astype(BF16)


def front_kernel(ncores, table, idx, observed, left_out, right_out, mats, sent_l, sent_r, got_l, got_r, pred,
                 sems):
    mine = lax.axis_index("cores")
    me = lax.axis_index("samp")
    count = idx.shape[1]
    step = 8 * R
    chunk = 256
    first, last = mine == 0, mine == ncores - 1
    barrier = pltpu.get_barrier_semaphore()

    @pl.when(mine > 0)
    def _():
        pl.semaphore_signal(barrier, inc=1, device_id=(mine - 1, me), device_id_type=MESH)

    @pl.when(mine < ncores - 1)
    def _():
        pl.semaphore_signal(barrier, inc=1, device_id=(mine + 1, me), device_id_type=MESH)

    onehot = picker(idx)

    def fill(t, _):
        at = pl.multiple_of(t * step, step)
        part = table[:, pl.ds(at, step)].T
        high, low = split(part)
        mats[pl.ds(at, step), :] = (jnp.dot(high, onehot, preferred_element_type=F32)
                                    + jnp.dot(low, onehot, preferred_element_type=F32))
        return 0

    lax.fori_loop(0, R // 8, fill, 0)
    pl.semaphore_wait(barrier, jnp.minimum(mine, 1) + jnp.minimum(ncores - 1 - mine, 1))
    unit = (lax.broadcasted_iota(jnp.int32, (R, count), 0) == 0).astype(F32)

    copy_l = pltpu.make_async_remote_copy(
        src_ref=sent_l, dst_ref=got_l, send_sem=sems.at[0], recv_sem=sems.at[1],
        device_id=(lax.rem(mine + 1, ncores), me), device_id_type=MESH)
    copy_r = pltpu.make_async_remote_copy(
        src_ref=sent_r, dst_ref=got_r, send_sem=sems.at[2], recv_sem=sems.at[3],
        device_id=(lax.rem(mine + ncores - 1, ncores), me), device_id_type=MESH)

    def go_left():
        @pl.when(first)
        def _():
            got_l[...] = unit
            sent_l[...] = mats[0:R, :]

        @pl.when(mine > 0)
        def _():
            copy_l.wait_recv()

            @pl.when(mine < ncores - 1)
            def _():
                for c in range(0, count, chunk):
                    def add(a, total):
                        return total + got_l[pl.ds(a, 1), c:c + chunk] * mats[pl.ds(pl.multiple_of(a * R, 8), R), c:c + chunk]
                    sent_l[:, c:c + chunk] = lax.fori_loop(0, R, add, jnp.zeros((R, chunk), F32), unroll=4)

        @pl.when(mine < ncores - 1)
        def _():
            copy_l.start()

    def go_right():
        @pl.when(last)
        def _():
            got_r[...] = unit

            def pick(a, _):
                sent_r[pl.ds(a, 1), :] = mats[pl.ds(pl.multiple_of(a * R, 8), 8), :][0:1, :]
                return 0
            lax.fori_loop(0, R, pick, 0)

        @pl.when(mine < ncores - 1)
        def _():
            copy_r.wait_recv()

            @pl.when(mine > 0)
            def _():
                for c in range(0, count, chunk):
                    def one(a, _):
                        m = mats[pl.ds(pl.multiple_of(a * R, 8), R), c:c + chunk] * got_r[:, c:c + chunk]
                        sent_r[pl.ds(a, 1), c:c + chunk] = jnp.sum(m, axis=0, keepdims=True)
                        return 0
                    lax.fori_loop(0, R, one, 0, unroll=4)

        @pl.when(mine > 0)
        def _():
            copy_r.start()

    @pl.when(2 * mine < ncores)
    def _():
        go_left()
        go_right()

    @pl.when(2 * mine >= ncores)
    def _():
        go_right()
        go_left()

    @pl.when(last)
    def _():
        pred[...] = jnp.sum(got_l[...] * sent_r[...], axis=0, keepdims=True)

    @pl.when(mine < ncores - 1)
    def _():
        pred[...] = jnp.sum(sent_l[...] * got_r[...], axis=0, keepdims=True)

    left_out[...] = got_l[...]
    right_out[...] = got_r[...] * (pred[...] - observed[...])

    @pl.when(mine < ncores - 1)
    def _():
        copy_l.wait_send()

    @pl.when(mine > 0)
    def _():
        copy_r.wait_send()


def gradient_kernel(ncores, nsamp, idx, left, right, grad, partial, got, small, got_small, esend, erecv, rsend, rrecv):
    mine = lax.axis_index("cores")
    me = lax.axis_index("samp")
    slab = grad.shape[0]
    half = slab // 2
    step = 8 * R
    wide = R * R // 2
    edge = jnp.logical_or(mine == 0, mine == ncores - 1)
    inner = jnp.logical_not(edge)
    barrier = pltpu.get_barrier_semaphore()
    for d in range(1, nsamp):
        pl.semaphore_signal(barrier, inc=1, device_id=(mine, lax.rem(me + d, nsamp)), device_id_type=MESH)
    onehot = picker(idx)
    nt = (((1,), (1,)), ((), ()))

    def against(vecs):
        high, low = split(vecs)
        return (lax.dot_general(onehot, high, nt, preferred_element_type=F32)
                + lax.dot_general(onehot, low, nt, preferred_element_type=F32))

    odd = lax.rem(me, 2)
    place = (1 - odd) * (me // 2) + odd * (nsamp - 1 - me // 2)

    def at_place(p):
        p = lax.rem(p + 2 * nsamp, nsamp)
        up = jnp.minimum(p // (nsamp // 2), 1)
        return (1 - up) * 2 * p + up * (2 * (nsamp - 1 - p) + 1)

    def ring(direction, c, t, peer):
        return pltpu.make_async_remote_copy(
            src_ref=got.at[direction, c, jnp.maximum(t - 1, 0)], dst_ref=got.at[direction, c, t],
            send_sem=rsend.at[direction, c, t], recv_sem=rrecv.at[direction, c, t],
            device_id=(mine, peer), device_id_type=MESH)

    def rows_of(direction, t):
        owner = at_place(place - 1 - t) if direction == 0 else at_place(place + 1 + t)
        return pl.ds(pl.multiple_of(owner * slab + direction * half, half), half)

    up_peer, down_peer = at_place(place + 1), at_place(place - 1)

    @pl.when(inner)
    def _():
        def block(t, _):
            lhs = left[pl.ds(pl.multiple_of(t * 8, 8), 8), :]
            outer = jnp.concatenate([lhs[a:a + 1, :] * right[...] for a in range(8)], axis=0)
            partial[:, pl.ds(pl.multiple_of(t * step, 128), step)] = against(outer)
            return 0
        lax.fori_loop(0, R // 8, block, 0)

    pl.semaphore_wait(barrier, nsamp - 1)

    @pl.when(inner)
    def _():
        peers = (up_peer, down_peer)
        for c in range(2):
            for direction in range(2):
                pltpu.make_async_remote_copy(
                    src_ref=partial.at[rows_of(direction, 0), pl.ds(c * wide, wide)], dst_ref=got.at[direction, c, 0],
                    send_sem=rsend.at[direction, c, 0], recv_sem=rrecv.at[direction, c, 0],
                    device_id=(mine, peers[direction]), device_id_type=MESH).start()

        def hop(t, _):
            for c in range(2):
                for direction in range(2):
                    ring(direction, c, t - 1, peers[direction]).wait_recv()
                    got[direction, c, t - 1] = (got[direction, c, t - 1]
                                                + partial[rows_of(direction, t), c * wide:c * wide + wide])
                    ring(direction, c, t, peers[direction]).start()
            return 0
        lax.fori_loop(1, nsamp - 1, hop, 0)
        end = nsamp - 2
        for c in range(2):
            for direction in range(2):
                ring(direction, c, end, peers[direction]).wait_recv()
                grad[direction * half:direction * half + half, c * wide:c * wide + wide] = (
                    got[direction, c, end] + partial[rows_of(direction, end + 1), c * wide:c * wide + wide])

        def drain(t, _):
            for c in range(2):
                for direction in range(2):
                    ring(direction, c, t, peers[direction]).wait_send()
            return 0
        lax.fori_loop(0, nsamp - 1, drain, 0)

    @pl.when(edge)
    def _():
        at_first = (mine == 0).astype(F32)
        vec = at_first * right[...] + (1.0 - at_first) * left[...] * right[0:1, :]
        pad = jnp.zeros((128 - R, vec.shape[1]), F32)
        small[...] = against(jnp.concatenate([vec, pad], axis=0))

        def send(d):
            to = lax.rem(me + d, nsamp)
            return pltpu.make_async_remote_copy(
                src_ref=small.at[pl.ds(pl.multiple_of(to * slab, slab), slab)], dst_ref=got_small.at[d - 1],
                send_sem=esend.at[d - 1], recv_sem=erecv.at[d - 1], device_id=(mine, to), device_id_type=MESH)
        for d in range(1, nsamp):
            send(d).start()
        total = small[pl.ds(pl.multiple_of(me * slab, slab), slab), :]
        for d in range(1, nsamp):
            send(d).wait_recv()
            total = total + got_small[d - 1]
        row = lax.broadcasted_iota(jnp.int32, (128, R * R), 0)
        col = lax.broadcasted_iota(jnp.int32, (128, R * R), 1)
        stride = 1 + (R - 1) * jnp.minimum(mine, 1)
        spread = jnp.where(jnp.logical_and(col == row * stride, row < R), 1.0, 0.0).astype(BF16)
        high, low = split(total)
        grad[...] = (jnp.dot(high, spread, preferred_element_type=F32)
                     + jnp.dot(low, spread, preferred_element_type=F32))
        for d in range(1, nsamp):
            send(d).wait_send()


def eliminate(mats):
    row = lax.broadcasted_iota(jnp.int32, (R, 128), 0)
    lane = lax.broadcasted_iota(jnp.int32, (R, 128), 1)
    mats = [jnp.concatenate([m, (row == lane).astype(F32)[:, :W]], axis=1) for m in mats]
    for j in range(R):
        nxt = []
        for m in mats:
            pivot = m[j:j + 1, :]
            scaled = pivot * (1.0 / pivot[:, j:j + 1])
            col = jnp.where(row[:, :1] > j, m[:, j:j + 1], 0.0)
            nxt.append(m - col * scaled)
        mats = nxt
    outs = []
    for m in mats:
        diag = jnp.sum(jnp.where(row == lane, m, 0.0), axis=1, keepdims=True)
        outs.append(m * lax.rsqrt(diag))
    return outs


def finish_kernel(pairs, uwide, hprev, hown, out):
    first, second = eliminate([hprev[...], hown[...]])
    carry = first[:, :W]
    inv = second[:, W:]
    tall = tall_of(weigh(carry, three(uwide[...])), pairs)
    pad = jnp.zeros((W - R, W), F32)
    inv = jnp.concatenate([inv, pad], axis=0)
    zero = jnp.zeros((W, W), F32)
    diag = jnp.concatenate([jnp.concatenate([inv, zero], axis=1), jnp.concatenate([zero, inv], axis=1)], axis=0)
    out[...] = lax.dot_general(tall, diag, (((1,), (1,)), ((), ())), precision=HIGH, preferred_element_type=F32)


def retract(updated, ncores, nsamp):
    slab = updated.shape[0]
    pairs = slab // 2
    vm = pl.BlockSpec(memory_space=pltpu.VMEM)
    uwide = jnp.pad(updated.reshape(slab, R, R).transpose(1, 0, 2), ((0, W - R), (0, 0), (0, W - R)))
    uwide = uwide.reshape(W, slab * W)
    square = jax.ShapeDtypeStruct((R, W), F32)
    hprev, hown = pl.pallas_call(
        functools.partial(gram_kernel, ncores, nsamp, pairs),
        out_shape=(square, square),
        in_specs=[vm],
        out_specs=(vm, vm),
        scratch_shapes=[
            pltpu.VMEM((R // 2, 128), F32),
            pltpu.VMEM((nsamp, R // 2, 128), F32),
            pltpu.VMEM((nsamp - 1, R // 2, 128), F32),
            pltpu.SemaphoreType.DMA((nsamp - 1,)),
            pltpu.SemaphoreType.DMA((nsamp,)),
            pltpu.SemaphoreType.DMA((nsamp - 1,)),
            pltpu.SemaphoreType.DMA((nsamp,)),
        ],
        compiler_params=pltpu.CompilerParams(collective_id=0, has_side_effects=True, vmem_limit_bytes=32 << 20),
        name="gram_chain",
    )(uwide)
    tall = pl.pallas_call(
        functools.partial(finish_kernel, pairs),
        out_shape=jax.ShapeDtypeStruct((pairs * R, 128), F32),
        in_specs=[vm] * 3,
        out_specs=vm,
        compiler_params=pltpu.CompilerParams(vmem_limit_bytes=32 << 20),
        name="finish",
    )(uwide, hprev, hown)
    tall = tall.reshape(pairs, R, 2, W)[..., :R]
    return tall.transpose(0, 2, 1, 3).reshape(slab, R * R)


def on_device(cores, indices, observed, step_size):
    ncores = lax.axis_size("cores")
    mine = lax.axis_index("cores")
    nsamp = lax.axis_size("samp")
    count = indices.shape[0]
    table = cores[0]
    own_index = lax.dynamic_index_in_dim(indices, mine, 1, keepdims=False)
    slab = N // nsamp
    first = lax.axis_index("samp") * slab
    vm = pl.BlockSpec(memory_space=pltpu.VMEM)
    vectors = jax.ShapeDtypeStruct((R, count), F32)
    left, right = pl.pallas_call(
        functools.partial(front_kernel, ncores),
        out_shape=(vectors, vectors),
        in_specs=[vm] * 3,
        out_specs=(vm, vm),
        scratch_shapes=[
            pltpu.VMEM((R * R, count), F32),
            pltpu.VMEM((R, count), F32),
            pltpu.VMEM((R, count), F32),
            pltpu.VMEM((R, count), F32),
            pltpu.VMEM((R, count), F32),
            pltpu.VMEM((1, count), F32),
            pltpu.SemaphoreType.DMA((4,)),
        ],
        compiler_params=pltpu.CompilerParams(collective_id=1, has_side_effects=True, vmem_limit_bytes=48 << 20),
        name="sample_vectors",
    )(table, own_index.reshape(1, count), observed.reshape(1, count))
    gradient = pl.pallas_call(
        functools.partial(gradient_kernel, ncores, nsamp),
        out_shape=jax.ShapeDtypeStruct((slab, R * R), F32),
        in_specs=[vm] * 3,
        out_specs=vm,
        scratch_shapes=[
            pltpu.VMEM((N, R * R), F32),
            pltpu.VMEM((2, 2, nsamp - 1, slab // 2, R * R // 2), F32),
            pltpu.VMEM((N, 128), F32),
            pltpu.VMEM((nsamp - 1, slab, 128), F32),
            pltpu.SemaphoreType.DMA((nsamp - 1,)),
            pltpu.SemaphoreType.DMA((nsamp - 1,)),
            pltpu.SemaphoreType.DMA((2, 2, nsamp - 1)),
            pltpu.SemaphoreType.DMA((2, 2, nsamp - 1)),
        ],
        compiler_params=pltpu.CompilerParams(collective_id=2, has_side_effects=True, vmem_limit_bytes=48 << 20),
        name="gradient_sum",
    )(own_index.reshape(1, count), left, right)
    kept = lax.dynamic_slice_in_dim(table, first, slab, 0)
    updated = kept - step_size * gradient
    return retract(updated, ncores, nsamp)[None]


def solution(mesh):
    in_specs = (P("cores", None, None), P("samp", None), P("samp"), P())
    out_specs = P("cores", "samp", None)
    return jax.shard_map(
        on_device, mesh=mesh, in_specs=in_specs, out_specs=out_specs, check_vma=False
    )
```

profile of v0, /device:TPU:4, one launch (start us, length us, event | category | flops | bytes accessed | tf_op | source)
XLA Modules:
  0.0 87.0 jit_solution(10287304048934665018)
XLA Ops:
  0.0 0.0 copy-start
  0.7 0.1 copy-done
  0.7 0.0 copy-start.1
  0.8 2.3 %copy-done.1 = f32[1,512,2304]{2,1,0:T(8,128)S(1)} copy-done((f32[1,512,2304]{2,1,0:T(8,128)S(1)}, f32[1,512,2304]{2,1,0:T(8,128)}, u32[]{:S(2)}) %copy-start.1) | copy-done | bytes 4718616
  3.1 0.0 copy-start.2
  3.1 0.7 copy-done.2
  3.8 13.2 %sample_vectors.1 = (f32[48,1024]{1,0:T(8,128)S(1)}, f32[48,1024]{1,0:T(8,128)S(1)}) custom-call(f32[512,2304]{1,0:T(8,128)S(1)} %bitcast.11, s32[1,1024]{1,0:T(1,128)S(1)} %dynamic-slice_bitcast_fusion.idx, f32[1,1024]{1,0:T(1,128)S(1)} %bitcast.12), custom_call_target="tpu_custom_call" | custom-call | tf_op jit(solution)/shard_map/sample_vectors/pallas_call | solution.py:431
  17.0 42.6 %gradient_sum.1 = f32[64,2304]{1,0:T(8,128)S(1)} custom-call(s32[1,1024]{1,0:T(1,128)S(1)} %dynamic-slice_bitcast_fusion.idx, f32[48,1024]{1,0:T(8,128)S(1)} %get-tuple-element.9.left, f32[48,1024]{1,0:T(8,128)S(1)} %get-tuple-element.10.right), custom_call_target="tpu_custom_call" | custom-call | tf_op jit(solution)/shard_map/gradient_sum/pallas_call | solution.py:448
  59.5 1.2 %bitcast_subtract_fusion = f32[64,2304]{1,0:T(8,128)S(1)} fusion(f32[64,2304]{1,0:T(8,128)S(1)} %gradient_sum.1, f32[1,512,2304]{2,1,0:T(8,128)} %param.4, s32[]{:T(128)S(6)} %select_n.7, f32[]{:T(128)S(6)} %copy.10), kind=kLoop, calls=%fused_computation.1 | loop fusion | flops 294912 | bytes 1769480 | tf_op jit(solution)/shard_map/sub | solution.py:467
  60.7 1.0 %reshape.20 = f32[64,48,48]{2,1,0:T(8,128)S(1)} reshape(f32[64,2304]{1,0:T(8,128)S(1)} %bitcast_subtract_fusion) | data formatting | bytes 1179648 | tf_op jit(solution)/shard_map/reshape | solution.py:388
  61.7 0.5 copy.9
  62.2 0.3 pad.4.clone
  62.5 0.7 reshape.21.uwide
  63.1 15.7 %gram_chain.1 = (f32[48,64]{1,0:T(8,128)S(1)}, f32[48,64]{1,0:T(8,128)S(1)}) custom-call(f32[64,4096]{1,0:T(8,128)S(1)} %reshape.21.uwide), custom_call_target="tpu_custom_call" | custom-call | tf_op jit(solution)/shard_map/gram_chain/pallas_call | solution.py:391
  78.8 5.6 %finish.1 = f32[1536,128]{1,0:T(8,128)S(1)} custom-call(f32[64,4096]{1,0:T(8,128)S(1)} %reshape.21.uwide, f32[48,64]{1,0:T(8,128)S(1)} %get-tuple-element.11.hprev, f32[48,64]{1,0:T(8,128)S(1)} %get-tuple-element.12.hown), custom_call_target="tpu_custom_call" | custom-call | tf_op jit(solution)/shard_map/finish/pallas_call | solution.py:408
  84.4 0.9 %reshape.22 = f32[32,48,2,64]{3,2,1,0:T(2,128)S(1)} reshape(f32[1536,128]{1,0:T(8,128)S(1)} %finish.1) | data formatting | bytes 1572864 | tf_op jit(solution)/shard_map/reshape | solution.py:416
  85.3 0.1 slice_bitcast_fusion
  85.4 0.1 copy.8
  85.5 1.5 %broadcast_in_dim_reshape.3 = f32[1,64,2304]{2,1,0:T(8,128)} reshape(f32[32,2,48,48]{3,2,1,0:T(8,128)S(1)} %copy.8) | data formatting | bytes 1179648 | tf_op jit(solution)/shard_map/broadcast_in_dim;reshape | solution.py:468
  (1 shorter events, 0.0 us)
Async XLA Ops:
  0.0 0.7 copy-start
  0.7 2.3 %copy-start.1 = (f32[1,512,2304]{2,1,0:T(8,128)S(1)}, f32[1,512,2304]{2,1,0:T(8,128)}, u32[]{:S(2)}) copy-start(f32[1,512,2304]{2,1,0:T(8,128)} %param.4) | copy-start | bytes 14155780
  3.1 0.7 copy-start.2
where the time goes:
time: 87.3 us; the launch traced here: 87 us
  Pallas kernels  77 us (88%)
  local copies, waits for them, and re-layouts  8.09 us (9%)
  other arithmetic  1.15 us (1%)
    pallas_call x1, Pallas kernels, on_device(): pl.pallas_call(functools.partial(gradient_kernel, ncores, nsamp), out_sha...  42.6 us
    pallas_call x1, Pallas kernels, retract(): pl.pallas_call(functools.partial(gram_kernel, ncores, nsamp, pairs), out_...  15.7 us
    pallas_call x1, Pallas kernels, on_device(): pl.pallas_call(functools.partial(front_kernel, ncores), out_shape=(vector...  13.2 us
    pallas_call x1, Pallas kernels, retract(): pl.pallas_call(functools.partial(finish_kernel, pairs), out_shape=jax.Sha...  5.62 us
    unnamed x7, local copies, waits for them, and re-layouts  3.6 us

commit v1 on v0

--- a/solution.py
+++ b/solution.py
@@ -56,8 +56,6 @@
         for d in range(nsamp):
             greet(mine - 1, lax.rem(me + d, nsamp))
 
-    pl.semaphore_wait(barrier, nsamp - 1 + nsamp * jnp.minimum(ncores - 1 - mine, 1))
-
     def own_copy(d):
         return pltpu.make_async_remote_copy(
             src_ref=sendbuf, dst_ref=got_own.at[d - 1], send_sem=send_own.at[d - 1],
@@ -90,6 +88,10 @@
             total = total + got_prev[d]
         hprev[...] = unpack(total)
 
+    @pl.when(jnp.logical_not(has_next))
+    def _():
+        pl.semaphore_wait(barrier, nsamp - 1)
+
     @pl.when(has_next)
     def _():
         before = hprev[...]
@@ -99,6 +101,7 @@
         both = both + jnp.dot(utl, wh, preferred_element_type=F32)
         gram = (both[:R, :W] + both[W:W + R, W:]) * (1.0 / N)
         sendbuf[...] = jnp.concatenate([gram[:R // 2], gram[R // 2:]], axis=1)
+        pl.semaphore_wait(barrier, 2 * nsamp - 1)
         for d in range(nsamp):
             next_copy(d).start()
         for d in range(1, nsamp):
@@ -120,16 +123,26 @@
     return jnp.where(row == idx_ref[...], 1.0, 0.0).astype(BF16)
 
 
-def front_kernel(ncores, table, idx, observed, left_out, right_out, mats, sent_l, sent_r, got_l, got_r, pred,
-                 sems):
+def front_kernel(ncores, cores, idx, observed, left_out, right_out, table, mats, sent_l, sent_r, got_l, got_r, pred,
+                 loads, sems):
     mine = lax.axis_index("cores")
     me = lax.axis_index("samp")
     count = idx.shape[1]
     step = 8 * R
+    blocks = R // 8
     chunk = 256
+    chunks = count // chunk
     first, last = mine == 0, mine == ncores - 1
+    inner = jnp.logical_not(jnp.logical_or(first, last))
     barrier = pltpu.get_barrier_semaphore()
 
+    def load(t):
+        lanes = pl.ds(pl.multiple_of(t * step, 128), step)
+        return pltpu.make_async_copy(cores.at[0, :, lanes], table.at[:, lanes], loads.at[t])
+
+    for t in range(blocks):
+        load(t).start()
+
     @pl.when(mine > 0)
     def _():
         pl.semaphore_signal(barrier, inc=1, device_id=(mine - 1, me), device_id_type=MESH)
@@ -139,83 +152,101 @@
         pl.semaphore_signal(barrier, inc=1, device_id=(mine + 1, me), device_id_type=MESH)
 
     onehot = picker(idx)
-
-    def fill(t, _):
-        at = pl.multiple_of(t * step, step)
-        part = table[:, pl.ds(at, step)].T
-        high, low = split(part)
-        mats[pl.ds(at, step), :] = (jnp.dot(high, onehot, preferred_element_type=F32)
-                                    + jnp.dot(low, onehot, preferred_element_type=F32))
-        return 0
-
-    lax.fori_loop(0, R // 8, fill, 0)
+    unit = (lax.broadcasted_iota(jnp.int32, (R, count), 0) == 0).astype(F32)
+
+    def picked(part):
+        high, low = split(part.T)
+        return (jnp.dot(high, onehot, preferred_element_type=F32)
+                + jnp.dot(low, onehot, preferred_element_type=F32))
+
+    @pl.when(first)
+    def _():
+        load(0).wait()
+        sent_l[...] = picked(table[:, 0:128])[0:R]
+        got_l[...] = unit
+        for t in range(1, blocks):
+            load(t).wait()
+
+    @pl.when(last)
+    def _():
+        for t in range(blocks):
+            load(t).wait()
+        row = lax.broadcasted_iota(jnp.int32, (R * R, 128), 0)
+        col = lax.broadcasted_iota(jnp.int32, (R * R, 128), 1)
+        heads = jnp.where(jnp.logical_and(row == col * R, col < R), 1.0, 0.0).astype(BF16)
+        high, low = split(table[...])
+        part = jnp.dot(high, heads, preferred_element_type=F32) + jnp.dot(low, heads, preferred_element_type=F32)
+        sent_r[...] = picked(part)[0:R]
+        got_r[...] = unit
+
+    @pl.when(inner)
+    def _():
+        def fill(t, _):
+            load(t).wait()
+            at = pl.multiple_of(t * step, step)
+            mats[pl.ds(at, step), :] = picked(table[:, pl.ds(at, step)])
+            return 0
+        lax.fori_loop(0, blocks, fill, 0)
+
     pl.semaphore_wait(barrier, jnp.minimum(mine, 1) + jnp.minimum(ncores - 1 - mine, 1))
-    unit = (lax.broadcasted_iota(jnp.int32, (R, count), 0) == 0).astype(F32)
-
-    copy_l = pltpu.make_async_remote_copy(
-        src_ref=sent_l, dst_ref=got_l, send_sem=sems.at[0], recv_sem=sems.at[1],
-        device_id=(lax.rem(mine + 1, ncores), me), device_id_type=MESH)
-    copy_r = pltpu.make_async_remote_copy(
-        src_ref=sent_r, dst_ref=got_r, send_sem=sems.at[2], recv_sem=sems.at[3],
-        device_id=(lax.rem(mine + ncores - 1, ncores), me), device_id_type=MESH)
-
-    def go_left():
-        @pl.when(first)
-        def _():
-            got_l[...] = unit
-            sent_l[...] = mats[0:R, :]
-
-        @pl.when(mine > 0)
-        def _():
-            copy_l.wait_recv()
-
-            @pl.when(mine < ncores - 1)
-            def _():
-                for c in range(0, count, chunk):
-                    def add(a, total):
-                        return total + got_l[pl.ds(a, 1), c:c + chunk] * mats[pl.ds(pl.multiple_of(a * R, 8), R), c:c + chunk]
-                    sent_l[:, c:c + chunk] = lax.fori_loop(0, R, add, jnp.zeros((R, chunk), F32), unroll=4)
-
-        @pl.when(mine < ncores - 1)
-        def _():
-            copy_l.start()
-
-    def go_right():
-        @pl.when(last)
-        def _():
-            got_r[...] = unit
-
-            def pick(a, _):
-                sent_r[pl.ds(a, 1), :] = mats[pl.ds(pl.multiple_of(a * R, 8), 8), :][0:1, :]
+
+    def copy_l(n):
+        lanes = pl.ds(n * chunk, chunk)
+        return pltpu.make_async_remote_copy(
+            src_ref=sent_l.at[:, lanes], dst_ref=got_l.at[:, lanes], send_sem=sems.at[0, n], recv_sem=sems.at[1, n],
+            device_id=(lax.rem(mine + 1, ncores), me), device_id_type=MESH)
+
+    def copy_r(n):
+        lanes = pl.ds(n * chunk, chunk)
+        return pltpu.make_async_remote_copy(
+            src_ref=sent_r.at[:, lanes], dst_ref=got_r.at[:, lanes], send_sem=sems.at[2, n], recv_sem=sems.at[3, n],
+            device_id=(lax.rem(mine + ncores - 1, ncores), me), device_id_type=MESH)
+
+    def pass_left():
+        for n in range(chunks):
+            c = n * chunk
+            copy_l(n).wait_recv()
+
+            def add(a, total):
+                return total + got_l[pl.ds(a, 1), c:c + chunk] * mats[pl.ds(pl.multiple_of(a * R, 8), R), c:c + chunk]
+            sent_l[:, c:c + chunk] = lax.fori_loop(0, R, add, jnp.zeros((R, chunk), F32), unroll=4)
+            copy_l(n).start()
+
+    def pass_right():
+        for n in range(chunks):
+            c = n * chunk
+            copy_r(n).wait_recv()
+
+            def one(a, _):
+                m = mats[pl.ds(pl.multiple_of(a * R, 8), R), c:c + chunk] * got_r[:, c:c + chunk]
+                sent_r[pl.ds(a, 1), c:c + chunk] = jnp.sum(m, axis=0, keepdims=True)
                 return 0
-            lax.fori_loop(0, R, pick, 0)
-
-        @pl.when(mine < ncores - 1)
-        def _():
-            copy_r.wait_recv()
-
-            @pl.when(mine > 0)
-            def _():
-                for c in range(0, count, chunk):
-                    def one(a, _):
-                        m = mats[pl.ds(pl.multiple_of(a * R, 8), R), c:c + chunk] * got_r[:, c:c + chunk]
-                        sent_r[pl.ds(a, 1), c:c + chunk] = jnp.sum(m, axis=0, keepdims=True)
-                        return 0
-                    lax.fori_loop(0, R, one, 0, unroll=4)
-
-        @pl.when(mine > 0)
-        def _():
-            copy_r.start()
-
-    @pl.when(2 * mine < ncores)
-    def _():
-        go_left()
-        go_right()
-
-    @pl.when(2 * mine >= ncores)
-    def _():
-        go_right()
-        go_left()
+            lax.fori_loop(0, R, one, 0, unroll=4)
+            copy_r(n).start()
+
+    @pl.when(first)
+    def _():
+        for n in range(chunks):
+            copy_l(n).start()
+        for n in range(chunks):
+            copy_r(n).wait_recv()
+
+    @pl.when(last)
+    def _():
+        for n in range(chunks):
+            copy_r(n).start()
+        for n in range(chunks):
+            copy_l(n).wait_recv()
+
+    @pl.when(jnp.logical_and(inner, 2 * mine < ncores))
+    def _():
+        pass_left()
+        pass_right()
+
+    @pl.when(jnp.logical_and(inner, 2 * mine >= ncores))
+    def _():
+        pass_right()
+        pass_left()
 
     @pl.when(last)
     def _():
@@ -230,25 +261,31 @@
 
     @pl.when(mine < ncores - 1)
     def _():
-        copy_l.wait_send()
+        for n in range(chunks):
+            copy_l(n).wait_send()
 
     @pl.when(mine > 0)
     def _():
-        copy_r.wait_send()
-
-
-def gradient_kernel(ncores, nsamp, idx, left, right, grad, partial, got, small, got_small, esend, erecv, rsend, rrecv):
+        for n in range(chunks):
+            copy_r(n).wait_send()
+
+
+def gradient_kernel(ncores, nsamp, idx, left, right, cores, rate, updated, partial, got, small, got_small, kept,
+                    ksem, esend, erecv, rsend, rrecv):
     mine = lax.axis_index("cores")
     me = lax.axis_index("samp")
-    slab = grad.shape[0]
+    slab = updated.shape[0]
     half = slab // 2
     step = 8 * R
-    wide = R * R // 2
+    parts = got.shape[1]
+    wide = R * R // parts
     edge = jnp.logical_or(mine == 0, mine == ncores - 1)
     inner = jnp.logical_not(edge)
     barrier = pltpu.get_barrier_semaphore()
     for d in range(1, nsamp):
         pl.semaphore_signal(barrier, inc=1, device_id=(mine, lax.rem(me + d, nsamp)), device_id_type=MESH)
+    keep = pltpu.make_async_copy(cores.at[0, pl.ds(pl.multiple_of(me * slab, slab), slab)], kept, ksem)
+    keep.start()
     onehot = picker(idx)
     nt = (((1,), (1,)), ((), ()))
 
@@ -277,45 +314,69 @@
 
     up_peer, down_peer = at_place(place + 1), at_place(place - 1)
 
+    def block(t, _):
+        lhs = left[pl.ds(pl.multiple_of(t * 8, 8), 8), :]
+        outer = jnp.concatenate([lhs[a:a + 1, :] * right[...] for a in range(8)], axis=0)
+        partial[:, pl.ds(pl.multiple_of(t * step, 128), step)] = against(outer)
+        return 0
+
+    each = R // 8 // parts
+
     @pl.when(inner)
     def _():
-        def block(t, _):
-            lhs = left[pl.ds(pl.multiple_of(t * 8, 8), 8), :]
-            outer = jnp.concatenate([lhs[a:a + 1, :] * right[...] for a in range(8)], axis=0)
-            partial[:, pl.ds(pl.multiple_of(t * step, 128), step)] = against(outer)
-            return 0
-        lax.fori_loop(0, R // 8, block, 0)
-
+        lax.fori_loop(0, each, block, 0)
+
+    keep.wait()
     pl.semaphore_wait(barrier, nsamp - 1)
 
     @pl.when(inner)
     def _():
         peers = (up_peer, down_peer)
-        for c in range(2):
+
+        def begin(c):
             for direction in range(2):
                 pltpu.make_async_remote_copy(
                     src_ref=partial.at[rows_of(direction, 0), pl.ds(c * wide, wide)], dst_ref=got.at[direction, c, 0],
                     send_sem=rsend.at[direction, c, 0], recv_sem=rrecv.at[direction, c, 0],
                     device_id=(mine, peers[direction]), device_id_type=MESH).start()
 
-        def hop(t, _):
-            for c in range(2):
-                for direction in range(2):
-                    ring(direction, c, t - 1, peers[direction]).wait_recv()
-                    got[direction, c, t - 1] = (got[direction, c, t - 1]
-                                                + partial[rows_of(direction, t), c * wide:c * wide + wide])
-                    ring(direction, c, t, peers[direction]).start()
-            return 0
-        lax.fori_loop(1, nsamp - 1, hop, 0)
-        end = nsamp - 2
-        for c in range(2):
+        def hop(c, t):
+            for direction in range(2):
+                ring(direction, c, t - 1, peers[direction]).wait_recv()
+                got[direction, c, t - 1] = (got[direction, c, t - 1]
+                                            + partial[rows_of(direction, t), c * wide:c * wide + wide])
+                ring(direction, c, t, peers[direction]).start()
+
+        def finish(c):
+            end = nsamp - 2
             for direction in range(2):
                 ring(direction, c, end, peers[direction]).wait_recv()
-                grad[direction * half:direction * half + half, c * wide:c * wide + wide] = (
+                here = (slice(direction * half, direction * half + half), slice(c * wide, c * wide + wide))
+                updated[here] = kept[here] - rate[0, 0] * (
                     got[direction, c, end] + partial[rows_of(direction, end + 1), c * wide:c * wide + wide])
 
+        for turn in range(parts):
+            if turn > 0:
+                lax.fori_loop(turn * each, (turn + 1) * each, block, 0)
+            begin(turn)
+            for c in range(turn):
+                if turn - c <= nsamp - 2:
+                    hop(c, turn - c)
+
+        def steady(turn, _):
+            for c in range(parts):
+                hop(c, turn - c)
+            return 0
+        lax.fori_loop(parts, nsamp - 1, steady, 0)
+        for turn in range(max(parts, nsamp - 1), parts + nsamp - 1):
+            for c in range(parts):
+                if turn - c <= nsamp - 2:
+                    hop(c, turn - c)
+                elif turn - c == nsamp - 1:
+                    finish(c)
+
         def drain(t, _):
-            for c in range(2):
+            for c in range(parts):
                 for direction in range(2):
                     ring(direction, c, t, peers[direction]).wait_send()
             return 0
@@ -344,8 +405,8 @@
         stride = 1 + (R - 1) * jnp.minimum(mine, 1)
         spread = jnp.where(jnp.logical_and(col == row * stride, row < R), 1.0, 0.0).astype(BF16)
         high, low = split(total)
-        grad[...] = (jnp.dot(high, spread, preferred_element_type=F32)
-                     + jnp.dot(low, spread, preferred_element_type=F32))
+        updated[...] = kept[...] - rate[0, 0] * (jnp.dot(high, spread, preferred_element_type=F32)
+                                                 + jnp.dot(low, spread, preferred_element_type=F32))
         for d in range(1, nsamp):
             send(d).wait_send()
 
@@ -354,13 +415,19 @@
     row = lax.broadcasted_iota(jnp.int32, (R, 128), 0)
     lane = lax.broadcasted_iota(jnp.int32, (R, 128), 1)
     mats = [jnp.concatenate([m, (row == lane).astype(F32)[:, :W]], axis=1) for m in mats]
-    for j in range(R):
+    for j in range(0, R, 2):
         nxt = []
         for m in mats:
-            pivot = m[j:j + 1, :]
-            scaled = pivot * (1.0 / pivot[:, j:j + 1])
-            col = jnp.where(row[:, :1] > j, m[:, j:j + 1], 0.0)
-            nxt.append(m - col * scaled)
+            col0 = jnp.broadcast_to(m[:, j:j + 1], (R, 128))
+            col1 = jnp.broadcast_to(m[:, j + 1:j + 2], (R, 128))
+            inv0 = 1.0 / col0[j:j + 1]
+            ratio = col0[j + 1:j + 2] * inv0
+            inv1 = 1.0 / (col1[j + 1:j + 2] - ratio * col0[j + 1:j + 2])
+            row0 = m[j:j + 1]
+            row1 = m[j + 1:j + 2] - ratio * row0
+            col1 = jnp.where(row > j + 1, col1 - col0 * ratio, 0.0)
+            col0 = jnp.where(row > j, col0, 0.0)
+            nxt.append(m - col0 * (row0 * inv0) - col1 * (row1 * inv1))
         mats = nxt
     outs = []
     for m in mats:
@@ -422,49 +489,50 @@
     mine = lax.axis_index("cores")
     nsamp = lax.axis_size("samp")
     count = indices.shape[0]
-    table = cores[0]
     own_index = lax.dynamic_index_in_dim(indices, mine, 1, keepdims=False)
     slab = N // nsamp
-    first = lax.axis_index("samp") * slab
+    parts = 3
     vm = pl.BlockSpec(memory_space=pltpu.VMEM)
     vectors = jax.ShapeDtypeStruct((R, count), F32)
     left, right = pl.pallas_call(
         functools.partial(front_kernel, ncores),
         out_shape=(vectors, vectors),
-        in_specs=[vm] * 3,
+        in_specs=[pl.BlockSpec(memory_space=pl.ANY), vm, vm],
         out_specs=(vm, vm),
         scratch_shapes=[
+            pltpu.VMEM((N, R * R), F32),
             pltpu.VMEM((R * R, count), F32),
             pltpu.VMEM((R, count), F32),
             pltpu.VMEM((R, count), F32),
             pltpu.VMEM((R, count), F32),
             pltpu.VMEM((R, count), F32),
             pltpu.VMEM((1, count), F32),
-            pltpu.SemaphoreType.DMA((4,)),
+            pltpu.SemaphoreType.DMA((R // 8,)),
+            pltpu.SemaphoreType.DMA((4, count // 256)),
         ],
         compiler_params=pltpu.CompilerParams(collective_id=1, has_side_effects=True, vmem_limit_bytes=48 << 20),
         name="sample_vectors",
-    )(table, own_index.reshape(1, count), observed.reshape(1, count))
-    gradient = pl.pallas_call(
+    )(cores, own_index.reshape(1, count), observed.reshape(1, count))
+    updated = pl.pallas_call(
         functools.partial(gradient_kernel, ncores, nsamp),
         out_shape=jax.ShapeDtypeStruct((slab, R * R), F32),
-        in_specs=[vm] * 3,
+        in_specs=[vm] * 3 + [pl.BlockSpec(memory_space=pl.ANY), pl.BlockSpec(memory_space=pltpu.SMEM)],
         out_specs=vm,
         scratch_shapes=[
             pltpu.VMEM((N, R * R), F32),
-            pltpu.VMEM((2, 2, nsamp - 1, slab // 2, R * R // 2), F32),
+            pltpu.VMEM((2, parts, nsamp - 1, slab // 2, R * R // parts), F32),
             pltpu.VMEM((N, 128), F32),
             pltpu.VMEM((nsamp - 1, slab, 128), F32),
+            pltpu.VMEM((slab, R * R), F32),
+            pltpu.SemaphoreType.DMA,
             pltpu.SemaphoreType.DMA((nsamp - 1,)),
             pltpu.SemaphoreType.DMA((nsamp - 1,)),
-            pltpu.SemaphoreType.DMA((2, 2, nsamp - 1)),
-            pltpu.SemaphoreType.DMA((2, 2, nsamp - 1)),
+            pltpu.SemaphoreType.DMA((2, parts, nsamp - 1)),
+            pltpu.SemaphoreType.DMA((2, parts, nsamp - 1)),
         ],
         compiler_params=pltpu.CompilerParams(collective_id=2, has_side_effects=True, vmem_limit_bytes=48 << 20),
         name="gradient_sum",
-    )(own_index.reshape(1, count), left, right)
-    kept = lax.dynamic_slice_in_dim(table, first, slab, 0)
-    updated = kept - step_size * gradient
+    )(own_index.reshape(1, count), left, right, cores, step_size.reshape(1, 1))
     return retract(updated, ncores, nsamp)[None]
 
 

time: 87.3 us -> 81.5 us (0.934)
  Pallas kernels: 77 us -> 72.4 us
  other arithmetic: 1.15 us -> 0 us
    pallas_call x1, Pallas kernels: 13.2 us -> 11 us  [on_device(): pl.pallas_call(functools.partial(front_kernel, ncores), out_shape=(vector...]
    pallas_call x1, Pallas kernels: 5.62 us -> 3.75 us  [retract(): pl.pallas_call(functools.partial(finish_kernel, pairs), out_shape=jax.Sha...]
    pallas_call x1, Pallas kernels: 15.7 us -> 14.4 us  [retract(): pl.pallas_call(functools.partial(gram_kernel, ncores, nsamp, pairs), out_...]
    sub x1 -> x0, other arithmetic: 1.15 us -> none  [on_device(): updated = kept - step_size * gradient]
where the time goes in v1:
time: 81.5 us; the launch traced here: 81.3 us
  Pallas kernels  72.4 us (89%)
  local copies, waits for them, and re-layouts  8.09 us (10%)
    pallas_call x1, Pallas kernels, on_device(): pl.pallas_call(functools.partial(gradient_kernel, ncores, nsamp), out_sha...  43.3 us
    pallas_call x1, Pallas kernels, retract(): pl.pallas_call(functools.partial(gram_kernel, ncores, nsamp, pairs), out_...  14.4 us
    pallas_call x1, Pallas kernels, on_device(): pl.pallas_call(functools.partial(front_kernel, ncores), out_shape=(vector...  11 us
    pallas_call x1, Pallas kernels, retract(): pl.pallas_call(functools.partial(finish_kernel, pairs), out_shape=jax.Sha...  3.75 us
    unnamed x7, local copies, waits for them, and re-layouts  3.6 us

profile of v1, /device:TPU:4, one launch (start us, length us, event | category | flops | bytes accessed | tf_op | source)
XLA Modules:
  0.0 81.3 jit_solution(2244908289868130001)
XLA Ops:
  0.0 0.0 copy-start
  0.7 0.1 copy-done
  0.7 0.0 copy-start.1
  0.8 2.3 %copy-done.1 = f32[1,512,2304]{2,1,0:T(8,128)S(1)} copy-done((f32[1,512,2304]{2,1,0:T(8,128)S(1)}, f32[1,512,2304]{2,1,0:T(8,128)}, u32[]{:S(2)}) %copy-start.1) | copy-done | bytes 4718616
  3.1 0.0 copy-start.2
  3.1 0.7 copy-done.2
  3.8 11.0 %sample_vectors.1 = (f32[48,1024]{1,0:T(8,128)S(1)}, f32[48,1024]{1,0:T(8,128)S(1)}) custom-call(f32[1,512,2304]{2,1,0:T(8,128)S(1)} %copy-done.1, s32[1,1024]{1,0:T(1,128)S(1)} %dynamic-slice_bitcast_fusion.idx, f32[1,1024]{1,0:T(1,128)S(1)} %bitcast.10), custom_call_target="tpu_custom_call" | custom-call | tf_op jit(solution)/shard_map/sample_vectors/pallas_call | solution.py:497
  14.8 43.3 %gradient_sum.1 = f32[64,2304]{1,0:T(8,128)S(1)} custom-call(s32[1,1024]{1,0:T(1,128)S(1)} %dynamic-slice_bitcast_fusion.idx, f32[48,1024]{1,0:T(8,128)S(1)} %get-tuple-element.9.left, f32[48,1024]{1,0:T(8,128)S(1)} %get-tuple-element.10.right, f32[1,512,2304]{2,1,0:T(8,128)S(1)} %copy-done.1, f32[1,1]{1,0:T(1,128)} %bitcast.9.rate), custom_call_target="tpu_custom_call" | custom-call | tf_op jit(solution)/shard_map/gradient_sum/pallas_call | solution.py:516
  58.1 1.0 %reshape.23 = f32[64,48,48]{2,1,0:T(8,128)S(1)} reshape(f32[64,2304]{1,0:T(8,128)S(1)} %gradient_sum.1) | data formatting | bytes 1179648 | tf_op jit(solution)/shard_map/reshape | solution.py:455
  59.0 0.5 copy.9
  59.6 0.3 pad.4.clone
  59.9 0.7 reshape.24.uwide
  60.5 14.4 %gram_chain.1 = (f32[48,64]{1,0:T(8,128)S(1)}, f32[48,64]{1,0:T(8,128)S(1)}) custom-call(f32[64,4096]{1,0:T(8,128)S(1)} %reshape.24.uwide), custom_call_target="tpu_custom_call" | custom-call | tf_op jit(solution)/shard_map/gram_chain/pallas_call | solution.py:458
  74.9 3.7 %finish.1 = f32[1536,128]{1,0:T(8,128)S(1)} custom-call(f32[64,4096]{1,0:T(8,128)S(1)} %reshape.24.uwide, f32[48,64]{1,0:T(8,128)S(1)} %get-tuple-element.11.hprev, f32[48,64]{1,0:T(8,128)S(1)} %get-tuple-element.12.hown), custom_call_target="tpu_custom_call" | custom-call | tf_op jit(solution)/shard_map/finish/pallas_call | solution.py:475
  78.7 0.9 %reshape.25 = f32[32,48,2,64]{3,2,1,0:T(2,128)S(1)} reshape(f32[1536,128]{1,0:T(8,128)S(1)} %finish.1) | data formatting | bytes 1572864 | tf_op jit(solution)/shard_map/reshape | solution.py:483
  79.6 0.1 slice_bitcast_fusion
  79.7 0.1 copy.8
  79.8 1.5 %broadcast_in_dim_reshape.3 = f32[1,64,2304]{2,1,0:T(8,128)} reshape(f32[32,2,48,48]{3,2,1,0:T(8,128)S(1)} %copy.8) | data formatting | bytes 1179648 | tf_op jit(solution)/shard_map/broadcast_in_dim;reshape | solution.py:536
  (1 shorter events, 0.0 us)
Async XLA Ops:
  0.0 0.7 copy-start
  0.7 2.3 %copy-start.1 = (f32[1,512,2304]{2,1,0:T(8,128)S(1)}, f32[1,512,2304]{2,1,0:T(8,128)}, u32[]{:S(2)}) copy-start(f32[1,512,2304]{2,1,0:T(8,128)} %cores.3) | copy-start | bytes 14155780
  3.1 0.7 copy-start.2

commit v2 on v1

--- a/solution.py
+++ b/solution.py
@@ -123,8 +123,8 @@
     return jnp.where(row == idx_ref[...], 1.0, 0.0).astype(BF16)
 
 
-def front_kernel(ncores, cores, idx, observed, left_out, right_out, table, mats, sent_l, sent_r, got_l, got_r, pred,
-                 loads, sems):
+def front_kernel(ncores, nsamp, room, cores, idx, every, observed, left_out, right_out, over, table, mats, sent_l, sent_r, got_l, got_r, pred,
+                 flag, got_flag, loads, sems, fsend, frecv):
     mine = lax.axis_index("cores")
     me = lax.axis_index("samp")
     count = idx.shape[1]
@@ -151,6 +151,22 @@
     def _():
         pl.semaphore_signal(barrier, inc=1, device_id=(mine + 1, me), device_id_type=MESH)
 
+    for d in range(1, nsamp):
+        pl.semaphore_signal(barrier, inc=1, device_id=(mine, lax.rem(me + d, nsamp)), device_id_type=MESH)
+
+    def tell(d):
+        return pltpu.make_async_remote_copy(
+            src_ref=flag, dst_ref=got_flag.at[d - 1], send_sem=fsend.at[d - 1], recv_sem=frecv.at[d - 1],
+            device_id=(mine, lax.rem(me + d, nsamp)), device_id_type=MESH)
+
+    most = jnp.zeros((nsamp, 1), F32)
+    owner = lax.broadcasted_iota(jnp.int32, (nsamp, count), 0)
+    for m in range(ncores):
+        member = jnp.where(every[m:m + 1, :] // (N // nsamp) == owner, 1.0, 0.0)
+        most = jnp.maximum(most, jnp.sum(member, axis=1, keepdims=True))
+    most = jnp.max(most, axis=0, keepdims=True)
+    flag[...] = jnp.broadcast_to(jnp.where(most > room, 1.0, 0.0), (8, 128))
+
     onehot = picker(idx)
     unit = (lax.broadcasted_iota(jnp.int32, (R, count), 0) == 0).astype(F32)
 
@@ -188,7 +204,9 @@
             return 0
         lax.fori_loop(0, blocks, fill, 0)
 
-    pl.semaphore_wait(barrier, jnp.minimum(mine, 1) + jnp.minimum(ncores - 1 - mine, 1))
+    pl.semaphore_wait(barrier, nsamp - 1 + jnp.minimum(mine, 1) + jnp.minimum(ncores - 1 - mine, 1))
+    for d in range(1, nsamp):
+        tell(d).start()
 
     def copy_l(n):
         lanes = pl.ds(n * chunk, chunk)
@@ -258,6 +276,13 @@
 
     left_out[...] = got_l[...]
     right_out[...] = got_r[...] * (pred[...] - observed[...])
+    worst = flag[...]
+    for d in range(1, nsamp):
+        tell(d).wait_recv()
+        worst = jnp.maximum(worst, got_flag[d - 1])
+    over[...] = worst
+    for d in range(1, nsamp):
+        tell(d).wait_send()
 
     @pl.when(mine < ncores - 1)
     def _():
@@ -268,6 +293,44 @@
     def _():
         for n in range(chunks):
             copy_r(n).wait_send()
+
+
+def against(onehot, vecs):
+    nt = (((1,), (1,)), ((), ()))
+    high, low = split(vecs)
+    return (lax.dot_general(onehot, high, nt, preferred_element_type=F32)
+            + lax.dot_general(onehot, low, nt, preferred_element_type=F32))
+
+
+def edge_gradient(nsamp, onehot, left, right, rate, updated, small, got_small, kept, esend, erecv):
+    mine = lax.axis_index("cores")
+    me = lax.axis_index("samp")
+    slab = updated.shape[0]
+    at_first = (mine == 0).astype(F32)
+    vec = at_first * right[...] + (1.0 - at_first) * left[...] * right[0:1, :]
+    pad = jnp.zeros((128 - R, vec.shape[1]), F32)
+    small[...] = against(onehot, jnp.concatenate([vec, pad], axis=0))
+
+    def send(d):
+        to = lax.rem(me + d, nsamp)
+        return pltpu.make_async_remote_copy(
+            src_ref=small.at[pl.ds(pl.multiple_of(to * slab, slab), slab)], dst_ref=got_small.at[d - 1],
+            send_sem=esend.at[d - 1], recv_sem=erecv.at[d - 1], device_id=(mine, to), device_id_type=MESH)
+    for d in range(1, nsamp):
+        send(d).start()
+    total = small[pl.ds(pl.multiple_of(me * slab, slab), slab), :]
+    for d in range(1, nsamp):
+        send(d).wait_recv()
+        total = total + got_small[d - 1]
+    row = lax.broadcasted_iota(jnp.int32, (128, R * R), 0)
+    col = lax.broadcasted_iota(jnp.int32, (128, R * R), 1)
+    stride = 1 + (R - 1) * jnp.minimum(mine, 1)
+    spread = jnp.where(jnp.logical_and(col == row * stride, row < R), 1.0, 0.0).astype(BF16)
+    high, low = split(total)
+    updated[...] = kept[...] - rate[0, 0] * (jnp.dot(high, spread, preferred_element_type=F32)
+                                             + jnp.dot(low, spread, preferred_element_type=F32))
+    for d in range(1, nsamp):
+        send(d).wait_send()
 
 
 def gradient_kernel(ncores, nsamp, idx, left, right, cores, rate, updated, partial, got, small, got_small, kept,
@@ -287,13 +350,6 @@
     keep = pltpu.make_async_copy(cores.at[0, pl.ds(pl.multiple_of(me * slab, slab), slab)], kept, ksem)
     keep.start()
     onehot = picker(idx)
-    nt = (((1,), (1,)), ((), ()))
-
-    def against(vecs):
-        high, low = split(vecs)
-        return (lax.dot_general(onehot, high, nt, preferred_element_type=F32)
-                + lax.dot_general(onehot, low, nt, preferred_element_type=F32))
-
     odd = lax.rem(me, 2)
     place = (1 - odd) * (me // 2) + odd * (nsamp - 1 - me // 2)
 
@@ -317,7 +373,7 @@
     def block(t, _):
         lhs = left[pl.ds(pl.multiple_of(t * 8, 8), 8), :]
         outer = jnp.concatenate([lhs[a:a + 1, :] * right[...] for a in range(8)], axis=0)
-        partial[:, pl.ds(pl.multiple_of(t * step, 128), step)] = against(outer)
+        partial[:, pl.ds(pl.multiple_of(t * step, 128), step)] = against(onehot, outer)
         return 0
 
     each = R // 8 // parts
@@ -384,29 +440,76 @@
 
     @pl.when(edge)
     def _():
-        at_first = (mine == 0).astype(F32)
-        vec = at_first * right[...] + (1.0 - at_first) * left[...] * right[0:1, :]
-        pad = jnp.zeros((128 - R, vec.shape[1]), F32)
-        small[...] = against(jnp.concatenate([vec, pad], axis=0))
+        edge_gradient(nsamp, onehot, left, right, rate, updated, small, got_small, kept, esend, erecv)
+
+
+def routed_kernel(ncores, nsamp, room, idx, left, right, cores, rate, updated, packed, got, small, got_small, kept,
+                  ksem, esend, erecv, psend, precv):
+    mine = lax.axis_index("cores")
+    me = lax.axis_index("samp")
+    count = idx.shape[1]
+    slab = updated.shape[0]
+    edge = jnp.logical_or(mine == 0, mine == ncores - 1)
+    barrier = pltpu.get_barrier_semaphore()
+    for d in range(1, nsamp):
+        pl.semaphore_signal(barrier, inc=1, device_id=(mine, lax.rem(me + d, nsamp)), device_id_type=MESH)
+    keep = pltpu.make_async_copy(cores.at[0, pl.ds(pl.multiple_of(me * slab, slab), slab)], kept, ksem)
+    keep.start()
+
+    @pl.when(edge)
+    def _():
+        keep.wait()
+        pl.semaphore_wait(barrier, nsamp - 1)
+        edge_gradient(nsamp, picker(idx), left, right, rate, updated, small, got_small, kept, esend, erecv)
+
+    @pl.when(jnp.logical_not(edge))
+    def _():
+        slab_of = idx[...] // slab
+        member = jnp.where(lax.broadcasted_iota(jnp.int32, (16, count), 0) == slab_of, 1.0, 0.0)
+        before = jnp.where(lax.broadcasted_iota(jnp.int32, (count, count), 0)
+                           < lax.broadcasted_iota(jnp.int32, (count, count), 1), 1.0, 0.0).astype(BF16)
+        earlier = jnp.dot(member.astype(BF16), before, preferred_element_type=F32)
+        place = slab_of * room + jnp.sum(member * earlier, axis=0, keepdims=True).astype(jnp.int32)
+        high, low = split(jnp.concatenate([left[...], right[...]], axis=0))
+        within = jnp.broadcast_to((idx[...] - slab_of * slab).astype(F32), (16, count)).astype(BF16)
+        rows = jnp.concatenate([high, low, within], axis=0)
+        spot = lax.broadcasted_iota(jnp.int32, (room, count), 0)
 
         def send(d):
+            return pltpu.make_async_remote_copy(
+                src_ref=packed.at[d], dst_ref=got.at[d], send_sem=psend.at[d], recv_sem=precv.at[d],
+                device_id=(mine, lax.rem(me + d, nsamp)), device_id_type=MESH)
+
+        def pack(d):
             to = lax.rem(me + d, nsamp)
-            return pltpu.make_async_remote_copy(
-                src_ref=small.at[pl.ds(pl.multiple_of(to * slab, slab), slab)], dst_ref=got_small.at[d - 1],
-                send_sem=esend.at[d - 1], recv_sem=erecv.at[d - 1], device_id=(mine, to), device_id_type=MESH)
-        for d in range(1, nsamp):
+            pick = jnp.where(spot == place - to * room, 1.0, 0.0).astype(BF16)
+            out = lax.dot_general(rows, pick, (((1,), (1,)), ((), ())), preferred_element_type=F32)
+            return jnp.concatenate([out[:2 * R] + out[2 * R:4 * R], out[4 * R:4 * R + 8]], axis=0)
+
+        def dispatch(d, _):
+            packed[d] = pack(d)
+
+            @pl.when(d == 1)
+            def _():
+                pl.semaphore_wait(barrier, nsamp - 1)
             send(d).start()
-        total = small[pl.ds(pl.multiple_of(me * slab, slab), slab), :]
-        for d in range(1, nsamp):
-            send(d).wait_recv()
-            total = total + got_small[d - 1]
-        row = lax.broadcasted_iota(jnp.int32, (128, R * R), 0)
-        col = lax.broadcasted_iota(jnp.int32, (128, R * R), 1)
-        stride = 1 + (R - 1) * jnp.minimum(mine, 1)
-        spread = jnp.where(jnp.logical_and(col == row * stride, row < R), 1.0, 0.0).astype(BF16)
-        high, low = split(total)
-        updated[...] = kept[...] - rate[0, 0] * (jnp.dot(high, spread, preferred_element_type=F32)
-                                                 + jnp.dot(low, spread, preferred_element_type=F32))
+            return 0
+        lax.fori_loop(1, nsamp, dispatch, 0)
+        got[0] = pack(0)
+        keep.wait()
+        group = count // room
+        step = 16 * R
+        for g in range(0, nsamp, group):
+            for d in range(max(g, 1), g + group):
+                send(d).wait_recv()
+            vecs = jnp.concatenate([got[d] for d in range(g, g + group)], axis=1)
+            ids = vecs[2 * R:2 * R + 1].astype(jnp.int32)
+            slices = jnp.where(lax.broadcasted_iota(jnp.int32, (slab, count), 0) == ids, 1.0, 0.0).astype(BF16)
+            for t in range(0, R, 16):
+                outer = jnp.concatenate([vecs[a:a + 1] * vecs[R:2 * R] for a in range(t, t + 16)], axis=0)
+                here = slice(t * R, t * R + step)
+                base = kept[:, here] if g == 0 else updated[:, here]
+                updated[:, here] = base - rate[0, 0] * against(slices, outer)
         for d in range(1, nsamp):
             send(d).wait_send()
 
@@ -492,13 +595,14 @@
     own_index = lax.dynamic_index_in_dim(indices, mine, 1, keepdims=False)
     slab = N // nsamp
     parts = 3
+    room = max(2 * count // nsamp, 128)
     vm = pl.BlockSpec(memory_space=pltpu.VMEM)
     vectors = jax.ShapeDtypeStruct((R, count), F32)
-    left, right = pl.pallas_call(
-        functools.partial(front_kernel, ncores),
-        out_shape=(vectors, vectors),
-        in_specs=[pl.BlockSpec(memory_space=pl.ANY), vm, vm],
-        out_specs=(vm, vm),
+    left, right, over = pl.pallas_call(
+        functools.partial(front_kernel, ncores, nsamp, room),
+        out_shape=(vectors, vectors, jax.ShapeDtypeStruct((8, 128), F32)),
+        in_specs=[pl.BlockSpec(memory_space=pl.ANY), vm, vm, vm],
+        out_specs=(vm, vm, vm),
         scratch_shapes=[
             pltpu.VMEM((N, R * R), F32),
             pltpu.VMEM((R * R, count), F32),
@@ -507,13 +611,17 @@
             pltpu.VMEM((R, count), F32),
             pltpu.VMEM((R, count), F32),
             pltpu.VMEM((1, count), F32),
+            pltpu.VMEM((8, 128), F32),
+            pltpu.VMEM((nsamp - 1, 8, 128), F32),
             pltpu.SemaphoreType.DMA((R // 8,)),
             pltpu.SemaphoreType.DMA((4, count // 256)),
+            pltpu.SemaphoreType.DMA((nsamp - 1,)),
+            pltpu.SemaphoreType.DMA((nsamp - 1,)),
         ],
         compiler_params=pltpu.CompilerParams(collective_id=1, has_side_effects=True, vmem_limit_bytes=48 << 20),
         name="sample_vectors",
-    )(cores, own_index.reshape(1, count), observed.reshape(1, count))
-    updated = pl.pallas_call(
+    )(cores, own_index.reshape(1, count), indices.T, observed.reshape(1, count))
+    summed = pl.pallas_call(
         functools.partial(gradient_kernel, ncores, nsamp),
         out_shape=jax.ShapeDtypeStruct((slab, R * R), F32),
         in_specs=[vm] * 3 + [pl.BlockSpec(memory_space=pl.ANY), pl.BlockSpec(memory_space=pltpu.SMEM)],
@@ -532,7 +640,29 @@
         ],
         compiler_params=pltpu.CompilerParams(collective_id=2, has_side_effects=True, vmem_limit_bytes=48 << 20),
         name="gradient_sum",
-    )(own_index.reshape(1, count), left, right, cores, step_size.reshape(1, 1))
+    )
+    routed = pl.pallas_call(
+        functools.partial(routed_kernel, ncores, nsamp, room),
+        out_shape=jax.ShapeDtypeStruct((slab, R * R), F32),
+        in_specs=[vm] * 3 + [pl.BlockSpec(memory_space=pl.ANY), pl.BlockSpec(memory_space=pltpu.SMEM)],
+        out_specs=vm,
+        scratch_shapes=[
+            pltpu.VMEM((nsamp, 2 * R + 8, room), F32),
+            pltpu.VMEM((nsamp, 2 * R + 8, room), F32),
+            pltpu.VMEM((N, 128), F32),
+            pltpu.VMEM((nsamp - 1, slab, 128), F32),
+            pltpu.VMEM((slab, R * R), F32),
+            pltpu.SemaphoreType.DMA,
+            pltpu.SemaphoreType.DMA((nsamp - 1,)),
+            pltpu.SemaphoreType.DMA((nsamp - 1,)),
+            pltpu.SemaphoreType.DMA((nsamp,)),
+            pltpu.SemaphoreType.DMA((nsamp,)),
+        ],
+        compiler_params=pltpu.CompilerParams(collective_id=3, has_side_effects=True, vmem_limit_bytes=48 << 20),
+        name="gradient_routed",
+    )
+    updated = lax.cond(over[0, 0] == 0.0, routed, summed,
+                       own_index.reshape(1, count), left, right, cores, step_size.reshape(1, 1))
     return retract(updated, ncores, nsamp)[None]
 
 

time: 81.5 us -> 68.7 us (0.84)
  Pallas kernels: 72.4 us -> 59.8 us
    pallas_call x2, Pallas kernels: 54.3 us -> 35.4 us  [the longest x1 21.3 us: on_device(): lax.cond(over[0, 0] == 0.0, routed, summed, own_index.reshape(1, count),...]
    pallas_call x1, Pallas kernels: 14.4 us -> 20.7 us  [retract(): pl.pallas_call(functools.partial(gram_kernel, ncores, nsamp, pairs), out_...]
    unnamed x7, local copies, waits for them, and re-layouts: 3.6 us -> 1.92 us
where the time goes in v2:
time: 68.7 us; the launch traced here: 68.3 us
  Pallas kernels  59.8 us (87%)
  local copies, waits for them, and re-layouts  7.57 us (11%)
  between operations  0.75 us (1%)
    pallas_call x1, Pallas kernels, on_device(): lax.cond(over[0, 0] == 0.0, routed, summed, own_index.reshape(1, count),...  21.3 us
    pallas_call x1, Pallas kernels, retract(): pl.pallas_call(functools.partial(gram_kernel, ncores, nsamp, pairs), out_...  20.7 us
    pallas_call x1, Pallas kernels, on_device(): pl.pallas_call(functools.partial(front_kernel, ncores, nsamp, room), out_...  14 us
    pallas_call x1, Pallas kernels, retract(): pl.pallas_call(functools.partial(finish_kernel, pairs), out_shape=jax.Sha...  3.74 us
    unnamed x7, local copies, waits for them, and re-layouts  1.92 us
    another operation x1, local copies, waits for them, and re-layouts, on_device(): return retract(updated, ncores, nsamp)[None]  1.48 us

profile of v2, /device:TPU:4, one launch (start us, length us, event | category | flops | bytes accessed | tf_op | source)
XLA Modules:
  0.0 68.3 jit_solution(656243448870647068)
XLA Ops:
  0.0 0.7 %dynamic-slice_bitcast_fusion.idx = s32[1,1024]{1,0:T(1,128)S(1)} fusion(s32[1024,4]{0,1:T(4,128)} %param.7, s32[]{:T(128)S(6)} %select_n.4), kind=kLoop, calls=%fused_computation.1 | loop fusion | bytes 8196 | tf_op jit(solution)/shard_map/reshape | solution.py:623
  0.7 0.0 copy-start
  0.7 0.7 %copy-done = s32[1024,4]{0,1:T(4,128)S(1)} copy-done((s32[1024,4]{0,1:T(4,128)S(1)}, s32[1024,4]{0,1:T(4,128)}, u32[]{:S(2)}) %copy-start) | copy-done | bytes 16408
  1.4 0.0 copy-start.1
  1.4 0.7 %copy-done.1 = f32[1024]{0:T(1024)S(1)} copy-done((f32[1024]{0:T(1024)S(1)}, f32[1024]{0:T(1024)}, u32[]{:S(2)}) %copy-start.1) | copy-done | bytes 4120
  2.1 0.0 copy-start.2
  2.1 14.0 %sample_vectors.1 = (f32[48,1024]{1,0:T(8,128)S(1)}, f32[48,1024]{1,0:T(8,128)S(1)}, f32[8,128]{1,0:T(8,128)S(1)}) custom-call(f32[1,512,2304]{2,1,0:T(8,128)} %cores.1, s32[1,1024]{1,0:T(1,128)S(1)} %dynamic-slice_bitcast_fusion.idx, s32[4,1024]{1,0:T(4,128)S(1)} %bitcast.11, f32[1,1024]{1,0:T(1,128)S(1)} %bitcast.12), custom_call_target="tpu_custom_call" | custom-call | tf_op jit(solution)/shard_map/sample_vectors/pallas_call | solution.py:601
  16.2 0.5 slice.6
  17.3 0.0 copy-done.2
  17.3 21.6 %conditional.1 = (f32[64,2304]{1,0:T(8,128)S(1)}) conditional(s32[]{:T(128)} %bitcast.3, (s32[1,1024]{1,0:T(1,128)S(1)}, f32[48,1024]{1,0:T(8,128)S(1)}, f32[48,1024]{1,0:T(8,128)S(1)}, f32[1,512,2304]{2,1,0:T(8,128)S(1)}, f32[1,1]{1,0:T(1,128)}) %tuple.14, (s32[1,1024]{1,0:T(1,128)S(1)}, f32[48,1024]{1,0:T(8,128)S(1)}, f32[48,1024]{1,0:T(8,128)S(1)}, ...), branch_computations={%region_0.1_spmd, %region_1.2_spmd} | conditional | bytes 8 | solution.py:664
  17.3 21.3 %gradient_routed.1 = f32[64,2304]{1,0:T(8,128)S(1)} custom-call(s32[1,1024]{1,0:T(1,128)S(1)} %get-tuple-element.33.idx, f32[48,1024]{1,0:T(8,128)S(1)} %get-tuple-element.34.left, f32[48,1024]{1,0:T(8,128)S(1)} %get-tuple-element.35.right, f32[1,512,2304]{2,1,0:T(8,128)S(1)} %get-tuple-element.36.cores, f32[1,1]{1,0:T(1,128)} %get-tuple-element.37.rate), custom_call_target="tpu_custom_call" | custom-call | tf_op jit(solution)/shard_map/cond/branch_1_fun/gradient_routed/pallas_call | solution.py:664
  38.9 1.0 %reshape.27 = f32[64,48,48]{2,1,0:T(8,128)S(1)} reshape(f32[64,2304]{1,0:T(8,128)S(1)} %get-tuple-element.48) | data formatting | bytes 1179648 | tf_op jit(solution)/shard_map/reshape | solution.py:558
  39.9 0.5 copy.9
  40.4 0.2 pad.4.clone
  40.6 0.7 reshape.28.uwide
  41.3 20.7 %gram_chain.1 = (f32[48,64]{1,0:T(8,128)S(1)}, f32[48,64]{1,0:T(8,128)S(1)}) custom-call(f32[64,4096]{1,0:T(8,128)S(1)} %reshape.28.uwide), custom_call_target="tpu_custom_call" | custom-call | tf_op jit(solution)/shard_map/gram_chain/pallas_call | solution.py:561
  62.0 3.7 %finish.1 = f32[1536,128]{1,0:T(8,128)S(1)} custom-call(f32[64,4096]{1,0:T(8,128)S(1)} %reshape.28.uwide, f32[48,64]{1,0:T(8,128)S(1)} %get-tuple-element.46.hprev, f32[48,64]{1,0:T(8,128)S(1)} %get-tuple-element.47.hown), custom_call_target="tpu_custom_call" | custom-call | tf_op jit(solution)/shard_map/finish/pallas_call | solution.py:578
  65.7 0.9 %reshape.29 = f32[32,48,2,64]{3,2,1,0:T(2,128)S(1)} reshape(f32[1536,128]{1,0:T(8,128)S(1)} %finish.1) | data formatting | bytes 1572864 | tf_op jit(solution)/shard_map/reshape | solution.py:586
  66.6 0.1 slice_bitcast_fusion
  66.7 0.1 copy.8
  66.8 1.5 %broadcast_in_dim_reshape.3 = f32[1,64,2304]{2,1,0:T(8,128)} reshape(f32[32,2,48,48]{3,2,1,0:T(8,128)S(1)} %copy.8) | data formatting | bytes 1179648 | tf_op jit(solution)/shard_map/broadcast_in_dim;reshape | solution.py:666
Async XLA Ops:
  0.7 0.7 %copy-start = (s32[1024,4]{0,1:T(4,128)S(1)}, s32[1024,4]{0,1:T(4,128)}, u32[]{:S(2)}) copy-start(s32[1024,4]{0,1:T(4,128)} %param.7) | copy-start | bytes 49156
  1.4 0.7 %copy-start.1 = (f32[1024]{0:T(1024)S(1)}, f32[1024]{0:T(1024)}, u32[]{:S(2)}) copy-start(f32[1024]{0:T(1024)} %param.8) | copy-start | bytes 12292
  2.1 15.2 %copy-start.2 = (f32[1,512,2304]{2,1,0:T(8,128)S(1)}, f32[1,512,2304]{2,1,0:T(8,128)}, u32[]{:S(2)}) copy-start(f32[1,512,2304]{2,1,0:T(8,128)} %cores.1) | copy-start | bytes 14155780

commit v3 on v2

--- a/solution.py
+++ b/solution.py
@@ -33,41 +33,47 @@
     return jnp.dot(jnp.concatenate([high, high, low], axis=1), ustack, preferred_element_type=F32)
 
 
-def tall_of(wide, pairs):
-    return jnp.concatenate([wide[:, 128 * p:128 * p + 128] for p in range(pairs)], axis=0)
-
-
-def gram_kernel(ncores, nsamp, pairs, uwide, hprev, hown, sendbuf, got_prev, got_own,
-                send_own, send_next, recv_own, recv_prev):
+def padded(x):
+    return jnp.concatenate([x, jnp.zeros((W - x.shape[0], x.shape[1]), F32)], axis=0)
+
+
+def across(ref, width):
+    return jnp.concatenate([ref[pl.ds(n, R, stride=R), :][:, :width] for n in range(R)], axis=1)
+
+
+def along(ref, width):
+    return jnp.concatenate([ref[R * n:R * n + R, :][:, :width] for n in range(R)], axis=1)
+
+
+def lay(ref, wide, width):
+    for n in range(R):
+        ref[R * n:R * n + R, 0:width] = wide[:, n * width:n * width + width]
+
+
+def greet_modes(barrier):
+    mine = lax.axis_index("cores")
+
+    @pl.when(mine > 0)
+    def _():
+        pl.semaphore_signal(barrier, inc=1, device_id=(mine - 1, lax.axis_index("samp")), device_id_type=MESH)
+
+
+def chain(ncores, nsamp, updated, hprev, hown, turned, moved, sendbuf, total_buf, got_prev, got_own,
+          send_own, recv_own, hop_sems):
     mine = lax.axis_index("cores")
     me = lax.axis_index("samp")
-    barrier = pltpu.get_barrier_semaphore()
+    slab = updated.shape[0]
     has_prev = mine > 0
     has_next = mine < ncores - 1
-
-    def greet(mode, other):
-        pl.semaphore_signal(barrier, inc=1, device_id=(mode, other), device_id_type=MESH)
-
-    for d in range(1, nsamp):
-        greet(mine, lax.rem(me + d, nsamp))
-
-    @pl.when(has_prev)
-    def _():
-        for d in range(nsamp):
-            greet(mine - 1, lax.rem(me + d, nsamp))
 
     def own_copy(d):
         return pltpu.make_async_remote_copy(
             src_ref=sendbuf, dst_ref=got_own.at[d - 1], send_sem=send_own.at[d - 1],
             recv_sem=recv_own.at[d - 1], device_id=(mine, lax.rem(me + d, nsamp)), device_id_type=MESH)
 
-    def next_copy(d):
-        return pltpu.make_async_remote_copy(
-            src_ref=sendbuf, dst_ref=got_prev.at[d], send_sem=send_next.at[d],
-            recv_sem=recv_prev.at[d], device_id=(mine + 1, lax.rem(me + d, nsamp)), device_id_type=MESH)
-
-    ustack = three(uwide[...])
-    uth, utl = split(tall_of(uwide[0:R, :], pairs).T)
+    onward = pltpu.make_async_remote_copy(
+        src_ref=total_buf, dst_ref=got_prev, send_sem=hop_sems.at[0], recv_sem=hop_sems.at[1],
+        device_id=(lax.rem(mine + 1, ncores), me), device_id_type=MESH)
 
     def unpack(x):
         return jnp.concatenate([x[:, :W], x[:, W:]], axis=0)
@@ -78,43 +84,42 @@
     hprev[...] = eye
     hown[...] = eye
 
-    @pl.when(has_prev)
-    def _():
-        total = jnp.zeros((R // 2, 128), F32)
-        for d in range(nsamp):
-            pltpu.make_async_remote_copy(
-                src_ref=sendbuf, dst_ref=got_prev.at[d], send_sem=send_next.at[d],
-                recv_sem=recv_prev.at[d], device_id=(mine, me), device_id_type=MESH).wait_recv()
-            total = total + got_prev[d]
-        hprev[...] = unpack(total)
-
-    @pl.when(jnp.logical_not(has_next))
-    def _():
-        pl.semaphore_wait(barrier, nsamp - 1)
-
     @pl.when(has_next)
     def _():
-        before = hprev[...]
-        wh, wl = split(tall_of(weigh(before, ustack), pairs))
-        both = jnp.dot(uth, wh, preferred_element_type=F32)
-        both = both + jnp.dot(uth, wl, preferred_element_type=F32)
-        both = both + jnp.dot(utl, wh, preferred_element_type=F32)
-        gram = (both[:R, :W] + both[W:W + R, W:]) * (1.0 / N)
+        turned[:, 0:slab] = updated[...].T
+        ustack = three(padded(across(turned, slab)))
+        zh, zl = split(along(turned, slab))
+
+        @pl.when(has_prev)
+        def _():
+            onward.wait_recv()
+            hprev[...] = unpack(got_prev[...])
+
+        lay(moved, weigh(hprev[...], ustack), slab)
+        yh, yl = split(across(moved, slab))
+        nt = (((1,), (1,)), ((), ()))
+        gram = lax.dot_general(zh, yh, nt, preferred_element_type=F32)
+        gram = gram + lax.dot_general(zh, yl, nt, preferred_element_type=F32)
+        gram = gram + lax.dot_general(zl, yh, nt, preferred_element_type=F32)
+        gram = jnp.concatenate([gram * (1.0 / N), jnp.zeros((R, W - R), F32)], axis=1)
         sendbuf[...] = jnp.concatenate([gram[:R // 2], gram[R // 2:]], axis=1)
-        pl.semaphore_wait(barrier, 2 * nsamp - 1)
-        for d in range(nsamp):
-            next_copy(d).start()
         for d in range(1, nsamp):
             own_copy(d).start()
         total = sendbuf[...]
         for d in range(1, nsamp):
             own_copy(d).wait_recv()
             total = total + got_own[d - 1]
+        total_buf[...] = total
+        onward.start()
         hown[...] = unpack(total)
-        for d in range(nsamp):
-            next_copy(d).wait_send()
         for d in range(1, nsamp):
             own_copy(d).wait_send()
+        onward.wait_send()
+
+    @pl.when(jnp.logical_not(has_next))
+    def _():
+        onward.wait_recv()
+        hprev[...] = unpack(got_prev[...])
 
 
 def picker(idx_ref):
@@ -333,8 +338,8 @@
         send(d).wait_send()
 
 
-def gradient_kernel(ncores, nsamp, idx, left, right, cores, rate, updated, partial, got, small, got_small, kept,
-                    ksem, esend, erecv, rsend, rrecv):
+def gradient_kernel(ncores, nsamp, idx, left, right, cores, rate, updated, hprev, hown, partial, got, small, got_small, kept,
+                    ksem, esend, erecv, rsend, rrecv, *links):
     mine = lax.axis_index("cores")
     me = lax.axis_index("samp")
     slab = updated.shape[0]
@@ -347,6 +352,7 @@
     barrier = pltpu.get_barrier_semaphore()
     for d in range(1, nsamp):
         pl.semaphore_signal(barrier, inc=1, device_id=(mine, lax.rem(me + d, nsamp)), device_id_type=MESH)
+    greet_modes(barrier)
     keep = pltpu.make_async_copy(cores.at[0, pl.ds(pl.multiple_of(me * slab, slab), slab)], kept, ksem)
     keep.start()
     onehot = picker(idx)
@@ -383,7 +389,7 @@
         lax.fori_loop(0, each, block, 0)
 
     keep.wait()
-    pl.semaphore_wait(barrier, nsamp - 1)
+    pl.semaphore_wait(barrier, nsamp - 1 + jnp.minimum(ncores - 1 - mine, 1))
 
     @pl.when(inner)
     def _():
@@ -442,9 +448,11 @@
     def _():
         edge_gradient(nsamp, onehot, left, right, rate, updated, small, got_small, kept, esend, erecv)
 
-
-def routed_kernel(ncores, nsamp, room, idx, left, right, cores, rate, updated, packed, got, small, got_small, kept,
-                  ksem, esend, erecv, psend, precv):
+    chain(ncores, nsamp, updated, hprev, hown, *links)
+
+
+def routed_kernel(ncores, nsamp, room, idx, left, right, cores, rate, updated, hprev, hown, packed, got, small, got_small, kept,
+                  ksem, esend, erecv, psend, precv, *links):
     mine = lax.axis_index("cores")
     me = lax.axis_index("samp")
     count = idx.shape[1]
@@ -453,13 +461,14 @@
     barrier = pltpu.get_barrier_semaphore()
     for d in range(1, nsamp):
         pl.semaphore_signal(barrier, inc=1, device_id=(mine, lax.rem(me + d, nsamp)), device_id_type=MESH)
+    greet_modes(barrier)
     keep = pltpu.make_async_copy(cores.at[0, pl.ds(pl.multiple_of(me * slab, slab), slab)], kept, ksem)
     keep.start()
 
     @pl.when(edge)
     def _():
         keep.wait()
-        pl.semaphore_wait(barrier, nsamp - 1)
+        pl.semaphore_wait(barrier, nsamp - 1 + jnp.minimum(ncores - 1 - mine, 1))
         edge_gradient(nsamp, picker(idx), left, right, rate, updated, small, got_small, kept, esend, erecv)
 
     @pl.when(jnp.logical_not(edge))
@@ -491,7 +500,7 @@
 
             @pl.when(d == 1)
             def _():
-                pl.semaphore_wait(barrier, nsamp - 1)
+                pl.semaphore_wait(barrier, nsamp - 1 + jnp.minimum(ncores - 1 - mine, 1))
             send(d).start()
             return 0
         lax.fori_loop(1, nsamp, dispatch, 0)
@@ -512,6 +521,8 @@
                 updated[:, here] = base - rate[0, 0] * against(slices, outer)
         for d in range(1, nsamp):
             send(d).wait_send()
+
+    chain(ncores, nsamp, updated, hprev, hown, *links)
 
 
 def eliminate(mats):
@@ -539,52 +550,15 @@
     return outs
 
 
-def finish_kernel(pairs, uwide, hprev, hown, out):
+def finish_kernel(updated, hprev, hown, out, turned, moved):
+    slab = updated.shape[0]
+    turned[:, 0:slab] = updated[...].T
+    ustack = three(padded(across(turned, slab)))
     first, second = eliminate([hprev[...], hown[...]])
-    carry = first[:, :W]
-    inv = second[:, W:]
-    tall = tall_of(weigh(carry, three(uwide[...])), pairs)
-    pad = jnp.zeros((W - R, W), F32)
-    inv = jnp.concatenate([inv, pad], axis=0)
-    zero = jnp.zeros((W, W), F32)
-    diag = jnp.concatenate([jnp.concatenate([inv, zero], axis=1), jnp.concatenate([zero, inv], axis=1)], axis=0)
-    out[...] = lax.dot_general(tall, diag, (((1,), (1,)), ((), ())), precision=HIGH, preferred_element_type=F32)
-
-
-def retract(updated, ncores, nsamp):
-    slab = updated.shape[0]
-    pairs = slab // 2
-    vm = pl.BlockSpec(memory_space=pltpu.VMEM)
-    uwide = jnp.pad(updated.reshape(slab, R, R).transpose(1, 0, 2), ((0, W - R), (0, 0), (0, W - R)))
-    uwide = uwide.reshape(W, slab * W)
-    square = jax.ShapeDtypeStruct((R, W), F32)
-    hprev, hown = pl.pallas_call(
-        functools.partial(gram_kernel, ncores, nsamp, pairs),
-        out_shape=(square, square),
-        in_specs=[vm],
-        out_specs=(vm, vm),
-        scratch_shapes=[
-            pltpu.VMEM((R // 2, 128), F32),
-            pltpu.VMEM((nsamp, R // 2, 128), F32),
-            pltpu.VMEM((nsamp - 1, R // 2, 128), F32),
-            pltpu.SemaphoreType.DMA((nsamp - 1,)),
-            pltpu.SemaphoreType.DMA((nsamp,)),
-            pltpu.SemaphoreType.DMA((nsamp - 1,)),
-            pltpu.SemaphoreType.DMA((nsamp,)),
-        ],
-        compiler_params=pltpu.CompilerParams(collective_id=0, has_side_effects=True, vmem_limit_bytes=32 << 20),
-        name="gram_chain",
-    )(uwide)
-    tall = pl.pallas_call(
-        functools.partial(finish_kernel, pairs),
-        out_shape=jax.ShapeDtypeStruct((pairs * R, 128), F32),
-        in_specs=[vm] * 3,
-        out_specs=vm,
-        compiler_params=pltpu.CompilerParams(vmem_limit_bytes=32 << 20),
-        name="finish",
-    )(uwide, hprev, hown)
-    tall = tall.reshape(pairs, R, 2, W)[..., :R]
-    return tall.transpose(0, 2, 1, 3).reshape(slab, R * R)
+    lay(moved, weigh(first[:, :W], ustack), slab)
+    ystack = three(padded(across(moved, slab)))
+    lay(turned, weigh(second[:, W:], ystack), slab)
+    out[...] = turned[:, 0:slab].T
 
 
 def on_device(cores, indices, observed, step_size):
@@ -621,11 +595,26 @@
         compiler_params=pltpu.CompilerParams(collective_id=1, has_side_effects=True, vmem_limit_bytes=48 << 20),
         name="sample_vectors",
     )(cores, own_index.reshape(1, count), indices.T, observed.reshape(1, count))
+    new_slices = jax.ShapeDtypeStruct((slab, R * R), F32)
+    square = jax.ShapeDtypeStruct((R, W), F32)
+    half = pltpu.VMEM((R // 2, 128), F32)
+    turning = pltpu.VMEM((R * R, 128), F32)
+    links = [
+        turning,
+        turning,
+        half,
+        half,
+        half,
+        pltpu.VMEM((nsamp - 1, R // 2, 128), F32),
+        pltpu.SemaphoreType.DMA((nsamp - 1,)),
+        pltpu.SemaphoreType.DMA((nsamp - 1,)),
+        pltpu.SemaphoreType.DMA((2,)),
+    ]
     summed = pl.pallas_call(
         functools.partial(gradient_kernel, ncores, nsamp),
-        out_shape=jax.ShapeDtypeStruct((slab, R * R), F32),
+        out_shape=(new_slices, square, square),
         in_specs=[vm] * 3 + [pl.BlockSpec(memory_space=pl.ANY), pl.BlockSpec(memory_space=pltpu.SMEM)],
-        out_specs=vm,
+        out_specs=(vm, vm, vm),
         scratch_shapes=[
             pltpu.VMEM((N, R * R), F32),
             pltpu.VMEM((2, parts, nsamp - 1, slab // 2, R * R // parts), F32),
@@ -637,15 +626,15 @@
             pltpu.SemaphoreType.DMA((nsamp - 1,)),
             pltpu.SemaphoreType.DMA((2, parts, nsamp - 1)),
             pltpu.SemaphoreType.DMA((2, parts, nsamp - 1)),
-        ],
+        ] + links,
         compiler_params=pltpu.CompilerParams(collective_id=2, has_side_effects=True, vmem_limit_bytes=48 << 20),
         name="gradient_sum",
     )
     routed = pl.pallas_call(
         functools.partial(routed_kernel, ncores, nsamp, room),
-        out_shape=jax.ShapeDtypeStruct((slab, R * R), F32),
+        out_shape=(new_slices, square, square),
         in_specs=[vm] * 3 + [pl.BlockSpec(memory_space=pl.ANY), pl.BlockSpec(memory_space=pltpu.SMEM)],
-        out_specs=vm,
+        out_specs=(vm, vm, vm),
         scratch_shapes=[
             pltpu.VMEM((nsamp, 2 * R + 8, room), F32),
             pltpu.VMEM((nsamp, 2 * R + 8, room), F32),
@@ -657,13 +646,22 @@
             pltpu.SemaphoreType.DMA((nsamp - 1,)),
             pltpu.SemaphoreType.DMA((nsamp,)),
             pltpu.SemaphoreType.DMA((nsamp,)),
-        ],
+        ] + links,
         compiler_params=pltpu.CompilerParams(collective_id=3, has_side_effects=True, vmem_limit_bytes=48 << 20),
         name="gradient_routed",
     )
-    updated = lax.cond(over[0, 0] == 0.0, routed, summed,
+    updated, hprev, hown = lax.cond(over[0, 0] == 0.0, routed, summed,
                        own_index.reshape(1, count), left, right, cores, step_size.reshape(1, 1))
-    return retract(updated, ncores, nsamp)[None]
+    result = pl.pallas_call(
+        finish_kernel,
+        out_shape=new_slices,
+        in_specs=[vm] * 3,
+        out_specs=vm,
+        scratch_shapes=[turning, turning],
+        compiler_params=pltpu.CompilerParams(vmem_limit_bytes=32 << 20),
+        name="finish",
+    )(updated, hprev, hown)
+    return result[None]
 
 
 def solution(mesh):

time: 68.7 us -> 64.9 us (0.945)
  local copies, waits for them, and re-layouts: 7.57 us -> 2.64 us
    pallas_call x1, Pallas kernels: 21.3 us -> 39.8 us  [on_device(): lax.cond(over[0, 0] == 0.0, routed, summed, own_index.reshape(1, count),...]
    pallas_call x2 -> x1, Pallas kernels: 24.4 us -> 6.59 us  [on_device(): pl.pallas_call(finish_kernel, out_shape=new_slices, in_specs=[vm] * 3, ou...]
    reshape x3 -> x0, local copies, waits for them, and re-layouts: 2.52 us -> none  [the longest x1 0.98 us: retract(): updated.reshape(slab, R, R).transpose(1, 0, 2)]
    another operation x1 -> x0, local copies, waits for them, and re-layouts: 1.48 us -> none  [on_device(): return retract(updated, ncores, nsamp)[None]]
    unnamed x7 -> x6, local copies, waits for them, and re-layouts: 1.92 us -> 1.41 us
where the time goes in v3:
time: 64.9 us; the launch traced here: 64 us
  Pallas kernels  60.4 us (93%)
  local copies, waits for them, and re-layouts  2.64 us (4%)
  between operations  0.68 us (1%)
    pallas_call x1, Pallas kernels, on_device(): lax.cond(over[0, 0] == 0.0, routed, summed, own_index.reshape(1, count),...  39.8 us
    pallas_call x1, Pallas kernels, on_device(): pl.pallas_call(functools.partial(front_kernel, ncores, nsamp, room), out_...  14 us
    pallas_call x1, Pallas kernels, on_device(): pl.pallas_call(finish_kernel, out_shape=new_slices, in_specs=[vm] * 3, ou...  6.59 us
    unnamed x6, local copies, waits for them, and re-layouts  1.41 us

profile of v3, /device:TPU:4, one launch (start us, length us, event | category | flops | bytes accessed | tf_op | source)
XLA Modules:
  0.0 64.0 jit_solution(15976059310795039638)
XLA Ops:
  0.0 0.7 %dynamic-slice_bitcast_fusion.idx = s32[1,1024]{1,0:T(1,128)S(1)} fusion(s32[1024,4]{0,1:T(4,128)} %param.7, s32[]{:T(128)S(6)} %select_n.4), kind=kLoop, calls=%fused_computation | loop fusion | bytes 8196 | tf_op jit(solution)/shard_map/reshape | solution.py:597
  0.7 0.0 copy-start
  0.7 0.7 %copy-done = s32[1024,4]{0,1:T(4,128)S(1)} copy-done((s32[1024,4]{0,1:T(4,128)S(1)}, s32[1024,4]{0,1:T(4,128)}, u32[]{:S(2)}) %copy-start) | copy-done | bytes 16408
  1.4 0.0 copy-start.1
  1.4 0.7 %copy-done.1 = f32[1024]{0:T(1024)S(1)} copy-done((f32[1024]{0:T(1024)S(1)}, f32[1024]{0:T(1024)}, u32[]{:S(2)}) %copy-start.1) | copy-done | bytes 4120
  2.1 0.0 copy-start.2
  2.1 14.0 %sample_vectors.1 = (f32[48,1024]{1,0:T(8,128)S(1)}, f32[48,1024]{1,0:T(8,128)S(1)}, f32[8,128]{1,0:T(8,128)S(1)}) custom-call(f32[1,512,2304]{2,1,0:T(8,128)} %cores.1, s32[1,1024]{1,0:T(1,128)S(1)} %dynamic-slice_bitcast_fusion.idx, s32[4,1024]{1,0:T(4,128)S(1)} %bitcast.7, f32[1,1024]{1,0:T(1,128)S(1)} %bitcast.8), custom_call_target="tpu_custom_call" | custom-call | tf_op jit(solution)/shard_map/sample_vectors/pallas_call | solution.py:575
  16.2 0.5 slice.3
  17.3 0.0 copy-done.2
  17.3 40.0 %conditional.1 = ((f32[64,2304]{1,0:T(8,128)S(1)}, f32[48,64]{1,0:T(8,128)S(1)}, f32[48,64]{1,0:T(8,128)S(1)})) conditional(s32[]{:T(128)} %bitcast.3, (s32[1,1024]{1,0:T(1,128)S(1)}, f32[48,1024]{1,0:T(8,128)S(1)}, f32[48,1024]{1,0:T(8,128)S(1)}, f32[1,512,2304]{2,1,0:T(8,128)S(1)}, f32[1,1]{1,0:T(1,128)}) %tuple.16, (s32[1,1024]{1,0:T(1,128)S(1)}, ...), branch_computations={%region_0.1_spmd, %region_1.2_spmd} | conditional | bytes 8 | solution.py:653
  17.3 39.8 %gradient_routed.1 = (f32[64,2304]{1,0:T(8,128)S(1)}, f32[48,64]{1,0:T(8,128)S(1)}, f32[48,64]{1,0:T(8,128)S(1)}) custom-call(s32[1,1024]{1,0:T(1,128)S(1)} %get-tuple-element.30.idx, f32[48,1024]{1,0:T(8,128)S(1)} %get-tuple-element.31.left, f32[48,1024]{1,0:T(8,128)S(1)} %get-tuple-element.32.right, f32[1,512,2304]{2,1,0:T(8,128)S(1)} %get-tuple-element.33.cores, ...), custom_call_target="tpu_custom_call" | custom-call | tf_op jit(solution)/shard_map/cond/branch_1_fun/gradient_routed/pallas_call | solution.py:653
  57.4 6.6 %finish.1 = f32[64,2304]{1,0:T(8,128)} custom-call(f32[64,2304]{1,0:T(8,128)S(1)} %get-tuple-element.44.updated, f32[48,64]{1,0:T(8,128)S(1)} %get-tuple-element.45.hprev, f32[48,64]{1,0:T(8,128)S(1)} %get-tuple-element.46.hown), custom_call_target="tpu_custom_call" | custom-call | tf_op jit(solution)/shard_map/finish/pallas_call | solution.py:655
Async XLA Ops:
  0.7 0.7 %copy-start = (s32[1024,4]{0,1:T(4,128)S(1)}, s32[1024,4]{0,1:T(4,128)}, u32[]{:S(2)}) copy-start(s32[1024,4]{0,1:T(4,128)} %param.7) | copy-start | bytes 49156
  1.4 0.7 %copy-start.1 = (f32[1024]{0:T(1024)S(1)}, f32[1024]{0:T(1024)}, u32[]{:S(2)}) copy-start(f32[1024]{0:T(1024)} %param.8) | copy-start | bytes 12292
  2.1 15.2 %copy-start.2 = (f32[1,512,2304]{2,1,0:T(8,128)S(1)}, f32[1,512,2304]{2,1,0:T(8,128)}, u32[]{:S(2)}) copy-start(f32[1,512,2304]{2,1,0:T(8,128)} %cores.1) | copy-start | bytes 14155780

commit v4 on v3

--- a/solution.py
+++ b/solution.py
@@ -50,19 +50,20 @@
         ref[R * n:R * n + R, 0:width] = wide[:, n * width:n * width + width]
 
 
-def greet_modes(barrier):
+def greet_modes(barrier, nsamp):
     mine = lax.axis_index("cores")
 
     @pl.when(mine > 0)
     def _():
-        pl.semaphore_signal(barrier, inc=1, device_id=(mine - 1, lax.axis_index("samp")), device_id_type=MESH)
-
-
-def chain(ncores, nsamp, updated, hprev, hown, turned, moved, sendbuf, total_buf, got_prev, got_own,
-          send_own, recv_own, hop_sems):
+        for d in range(nsamp):
+            pl.semaphore_signal(barrier, inc=1, device_id=(mine - 1, lax.rem(lax.axis_index("samp") + d, nsamp)),
+                                device_id_type=MESH)
+
+
+def chain(ncores, nsamp, slab, turned, hprev, hown, moved, sendbuf, got_prev, got_own,
+          send_own, recv_own, send_next, recv_prev):
     mine = lax.axis_index("cores")
     me = lax.axis_index("samp")
-    slab = updated.shape[0]
     has_prev = mine > 0
     has_next = mine < ncores - 1
 
@@ -71,9 +72,17 @@
             src_ref=sendbuf, dst_ref=got_own.at[d - 1], send_sem=send_own.at[d - 1],
             recv_sem=recv_own.at[d - 1], device_id=(mine, lax.rem(me + d, nsamp)), device_id_type=MESH)
 
-    onward = pltpu.make_async_remote_copy(
-        src_ref=total_buf, dst_ref=got_prev, send_sem=hop_sems.at[0], recv_sem=hop_sems.at[1],
-        device_id=(lax.rem(mine + 1, ncores), me), device_id_type=MESH)
+    def next_copy(d):
+        return pltpu.make_async_remote_copy(
+            src_ref=sendbuf, dst_ref=got_prev.at[d], send_sem=send_next.at[d], recv_sem=recv_prev.at[d],
+            device_id=(lax.rem(mine + 1, ncores), lax.rem(me + d, nsamp)), device_id_type=MESH)
+
+    def take_prev():
+        total = jnp.zeros((R // 2, 128), F32)
+        for d in range(nsamp):
+            next_copy(d).wait_recv()
+            total = total + got_prev[d]
+        hprev[...] = unpack(total)
 
     def unpack(x):
         return jnp.concatenate([x[:, :W], x[:, W:]], axis=0)
@@ -86,14 +95,12 @@
 
     @pl.when(has_next)
     def _():
-        turned[:, 0:slab] = updated[...].T
         ustack = three(padded(across(turned, slab)))
         zh, zl = split(along(turned, slab))
 
         @pl.when(has_prev)
         def _():
-            onward.wait_recv()
-            hprev[...] = unpack(got_prev[...])
+            take_prev()
 
         lay(moved, weigh(hprev[...], ustack), slab)
         yh, yl = split(across(moved, slab))
@@ -103,23 +110,23 @@
         gram = gram + lax.dot_general(zl, yh, nt, preferred_element_type=F32)
         gram = jnp.concatenate([gram * (1.0 / N), jnp.zeros((R, W - R), F32)], axis=1)
         sendbuf[...] = jnp.concatenate([gram[:R // 2], gram[R // 2:]], axis=1)
+        for d in range(nsamp):
+            next_copy(d).start()
         for d in range(1, nsamp):
             own_copy(d).start()
         total = sendbuf[...]
         for d in range(1, nsamp):
             own_copy(d).wait_recv()
             total = total + got_own[d - 1]
-        total_buf[...] = total
-        onward.start()
         hown[...] = unpack(total)
         for d in range(1, nsamp):
             own_copy(d).wait_send()
-        onward.wait_send()
+        for d in range(nsamp):
+            next_copy(d).wait_send()
 
     @pl.when(jnp.logical_not(has_next))
     def _():
-        onward.wait_recv()
-        hprev[...] = unpack(got_prev[...])
+        take_prev()
 
 
 def picker(idx_ref):
@@ -338,10 +345,11 @@
         send(d).wait_send()
 
 
-def gradient_kernel(ncores, nsamp, idx, left, right, cores, rate, updated, hprev, hown, partial, got, small, got_small, kept,
+def gradient_kernel(ncores, nsamp, idx, left, right, cores, rate, turned, hprev, hown, partial, got, small, got_small, kept,
                     ksem, esend, erecv, rsend, rrecv, *links):
     mine = lax.axis_index("cores")
     me = lax.axis_index("samp")
+    updated, links = links[0], links[1:]
     slab = updated.shape[0]
     half = slab // 2
     step = 8 * R
@@ -352,7 +360,7 @@
     barrier = pltpu.get_barrier_semaphore()
     for d in range(1, nsamp):
         pl.semaphore_signal(barrier, inc=1, device_id=(mine, lax.rem(me + d, nsamp)), device_id_type=MESH)
-    greet_modes(barrier)
+    greet_modes(barrier, nsamp)
     keep = pltpu.make_async_copy(cores.at[0, pl.ds(pl.multiple_of(me * slab, slab), slab)], kept, ksem)
     keep.start()
     onehot = picker(idx)
@@ -389,7 +397,7 @@
         lax.fori_loop(0, each, block, 0)
 
     keep.wait()
-    pl.semaphore_wait(barrier, nsamp - 1 + jnp.minimum(ncores - 1 - mine, 1))
+    pl.semaphore_wait(barrier, nsamp - 1 + nsamp * jnp.minimum(ncores - 1 - mine, 1))
 
     @pl.when(inner)
     def _():
@@ -448,28 +456,31 @@
     def _():
         edge_gradient(nsamp, onehot, left, right, rate, updated, small, got_small, kept, esend, erecv)
 
-    chain(ncores, nsamp, updated, hprev, hown, *links)
-
-
-def routed_kernel(ncores, nsamp, room, idx, left, right, cores, rate, updated, hprev, hown, packed, got, small, got_small, kept,
+    turned[:, 0:slab] = updated[...].T
+    chain(ncores, nsamp, slab, turned, hprev, hown, *links)
+
+
+def routed_kernel(ncores, nsamp, room, idx, left, right, cores, rate, turned, hprev, hown, packed, got, small, got_small, kept,
                   ksem, esend, erecv, psend, precv, *links):
     mine = lax.axis_index("cores")
     me = lax.axis_index("samp")
     count = idx.shape[1]
+    updated, links = links[0], links[1:]
     slab = updated.shape[0]
     edge = jnp.logical_or(mine == 0, mine == ncores - 1)
     barrier = pltpu.get_barrier_semaphore()
     for d in range(1, nsamp):
         pl.semaphore_signal(barrier, inc=1, device_id=(mine, lax.rem(me + d, nsamp)), device_id_type=MESH)
-    greet_modes(barrier)
+    greet_modes(barrier, nsamp)
     keep = pltpu.make_async_copy(cores.at[0, pl.ds(pl.multiple_of(me * slab, slab), slab)], kept, ksem)
     keep.start()
 
     @pl.when(edge)
     def _():
         keep.wait()
-        pl.semaphore_wait(barrier, nsamp - 1 + jnp.minimum(ncores - 1 - mine, 1))
+        pl.semaphore_wait(barrier, nsamp - 1 + nsamp * jnp.minimum(ncores - 1 - mine, 1))
         edge_gradient(nsamp, picker(idx), left, right, rate, updated, small, got_small, kept, esend, erecv)
+        turned[:, 0:slab] = updated[...].T
 
     @pl.when(jnp.logical_not(edge))
     def _():
@@ -500,12 +511,14 @@
 
             @pl.when(d == 1)
             def _():
-                pl.semaphore_wait(barrier, nsamp - 1 + jnp.minimum(ncores - 1 - mine, 1))
+                pl.semaphore_wait(barrier, nsamp - 1 + nsamp * jnp.minimum(ncores - 1 - mine, 1))
             send(d).start()
             return 0
         lax.fori_loop(1, nsamp, dispatch, 0)
         got[0] = pack(0)
         keep.wait()
+        turned[:, 0:slab] = kept[...].T
+        nt = (((1,), (1,)), ((), ()))
         group = count // room
         step = 16 * R
         for g in range(0, nsamp, group):
@@ -516,13 +529,15 @@
             slices = jnp.where(lax.broadcasted_iota(jnp.int32, (slab, count), 0) == ids, 1.0, 0.0).astype(BF16)
             for t in range(0, R, 16):
                 outer = jnp.concatenate([vecs[a:a + 1] * vecs[R:2 * R] for a in range(t, t + 16)], axis=0)
+                high, low = split(outer)
                 here = slice(t * R, t * R + step)
-                base = kept[:, here] if g == 0 else updated[:, here]
-                updated[:, here] = base - rate[0, 0] * against(slices, outer)
+                turned[here, 0:slab] = turned[here, 0:slab] - rate[0, 0] * (
+                    lax.dot_general(high, slices, nt, preferred_element_type=F32)
+                    + lax.dot_general(low, slices, nt, preferred_element_type=F32))
         for d in range(1, nsamp):
             send(d).wait_send()
 
-    chain(ncores, nsamp, updated, hprev, hown, *links)
+    chain(ncores, nsamp, slab, turned, hprev, hown, *links)
 
 
 def eliminate(mats):
@@ -550,15 +565,14 @@
     return outs
 
 
-def finish_kernel(updated, hprev, hown, out, turned, moved):
-    slab = updated.shape[0]
-    turned[:, 0:slab] = updated[...].T
+def finish_kernel(turned, hprev, hown, out, last, moved):
+    slab = out.shape[0]
     ustack = three(padded(across(turned, slab)))
     first, second = eliminate([hprev[...], hown[...]])
     lay(moved, weigh(first[:, :W], ustack), slab)
     ystack = three(padded(across(moved, slab)))
-    lay(turned, weigh(second[:, W:], ystack), slab)
-    out[...] = turned[:, 0:slab].T
+    lay(last, weigh(second[:, W:], ystack), slab)
+    out[...] = last[:, 0:slab].T
 
 
 def on_device(cores, indices, observed, step_size):
@@ -597,22 +611,21 @@
     )(cores, own_index.reshape(1, count), indices.T, observed.reshape(1, count))
     new_slices = jax.ShapeDtypeStruct((slab, R * R), F32)
     square = jax.ShapeDtypeStruct((R, W), F32)
-    half = pltpu.VMEM((R // 2, 128), F32)
     turning = pltpu.VMEM((R * R, 128), F32)
     links = [
+        pltpu.VMEM((slab, R * R), F32),
         turning,
-        turning,
-        half,
-        half,
-        half,
+        pltpu.VMEM((R // 2, 128), F32),
+        pltpu.VMEM((nsamp, R // 2, 128), F32),
         pltpu.VMEM((nsamp - 1, R // 2, 128), F32),
         pltpu.SemaphoreType.DMA((nsamp - 1,)),
         pltpu.SemaphoreType.DMA((nsamp - 1,)),
-        pltpu.SemaphoreType.DMA((2,)),
+        pltpu.SemaphoreType.DMA((nsamp,)),
+        pltpu.SemaphoreType.DMA((nsamp,)),
     ]
     summed = pl.pallas_call(
         functools.partial(gradient_kernel, ncores, nsamp),
-        out_shape=(new_slices, square, square),
+        out_shape=(jax.ShapeDtypeStruct((R * R, 128), F32), square, square),
         in_specs=[vm] * 3 + [pl.BlockSpec(memory_space=pl.ANY), pl.BlockSpec(memory_space=pltpu.SMEM)],
         out_specs=(vm, vm, vm),
         scratch_shapes=[
@@ -632,7 +645,7 @@
     )
     routed = pl.pallas_call(
         functools.partial(routed_kernel, ncores, nsamp, room),
-        out_shape=(new_slices, square, square),
+        out_shape=(jax.ShapeDtypeStruct((R * R, 128), F32), square, square),
         in_specs=[vm] * 3 + [pl.BlockSpec(memory_space=pl.ANY), pl.BlockSpec(memory_space=pltpu.SMEM)],
         out_specs=(vm, vm, vm),
         scratch_shapes=[

time: 64.9 us -> 60.7 us (0.935)
  Pallas kernels: 60.4 us -> 56.8 us
    pallas_call x1, Pallas kernels: 39.8 us -> 37.4 us  [on_device(): lax.cond(over[0, 0] == 0.0, routed, summed, own_index.reshape(1, count),...]
    pallas_call x1, Pallas kernels: 6.59 us -> 5.4 us  [on_device(): pl.pallas_call(finish_kernel, out_shape=new_slices, in_specs=[vm] * 3, ou...]
where the time goes in v4:
time: 60.7 us; the launch traced here: 60.4 us
  Pallas kernels  56.8 us (94%)
  local copies, waits for them, and re-layouts  2.64 us (4%)
  between operations  0.68 us (1%)
    pallas_call x1, Pallas kernels, on_device(): lax.cond(over[0, 0] == 0.0, routed, summed, own_index.reshape(1, count),...  37.4 us
    pallas_call x1, Pallas kernels, on_device(): pl.pallas_call(functools.partial(front_kernel, ncores, nsamp, room), out_...  14 us
    pallas_call x1, Pallas kernels, on_device(): pl.pallas_call(finish_kernel, out_shape=new_slices, in_specs=[vm] * 3, ou...  5.4 us
    unnamed x6, local copies, waits for them, and re-layouts  1.41 us

profile of v4, /device:TPU:4, one launch (start us, length us, event | category | flops | bytes accessed | tf_op | source)
XLA Modules:
  0.0 60.4 jit_solution(2499430696562455768)
XLA Ops:
  0.0 0.7 %dynamic-slice_bitcast_fusion.idx = s32[1,1024]{1,0:T(1,128)S(1)} fusion(s32[1024,4]{0,1:T(4,128)} %param.7, s32[]{:T(128)S(6)} %select_n.4), kind=kLoop, calls=%fused_computation | loop fusion | bytes 8196 | tf_op jit(solution)/shard_map/reshape | solution.py:611
  0.7 0.0 copy-start
  0.7 0.7 %copy-done = s32[1024,4]{0,1:T(4,128)S(1)} copy-done((s32[1024,4]{0,1:T(4,128)S(1)}, s32[1024,4]{0,1:T(4,128)}, u32[]{:S(2)}) %copy-start) | copy-done | bytes 16408
  1.4 0.0 copy-start.1
  1.4 0.7 %copy-done.1 = f32[1024]{0:T(1024)S(1)} copy-done((f32[1024]{0:T(1024)S(1)}, f32[1024]{0:T(1024)}, u32[]{:S(2)}) %copy-start.1) | copy-done | bytes 4120
  2.1 0.0 copy-start.2
  2.1 14.0 %sample_vectors.1 = (f32[48,1024]{1,0:T(8,128)S(1)}, f32[48,1024]{1,0:T(8,128)S(1)}, f32[8,128]{1,0:T(8,128)S(1)}) custom-call(f32[1,512,2304]{2,1,0:T(8,128)} %cores.1, s32[1,1024]{1,0:T(1,128)S(1)} %dynamic-slice_bitcast_fusion.idx, s32[4,1024]{1,0:T(4,128)S(1)} %bitcast.7, f32[1,1024]{1,0:T(1,128)S(1)} %bitcast.8), custom_call_target="tpu_custom_call" | custom-call | tf_op jit(solution)/shard_map/sample_vectors/pallas_call | solution.py:589
  16.2 0.5 slice.3
  17.3 0.0 copy-done.2
  17.3 37.6 %conditional.1 = ((f32[2304,128]{1,0:T(8,128)S(1)}, f32[48,64]{1,0:T(8,128)S(1)}, f32[48,64]{1,0:T(8,128)S(1)})) conditional(s32[]{:T(128)} %bitcast.3, (s32[1,1024]{1,0:T(1,128)S(1)}, f32[48,1024]{1,0:T(8,128)S(1)}, f32[48,1024]{1,0:T(8,128)S(1)}, f32[1,512,2304]{2,1,0:T(8,128)S(1)}, f32[1,1]{1,0:T(1,128)}) %tuple.16, (s32[1,1024]{1,0:T(1,128)S(1)}, ...), branch_computations={%region_0.1_spmd, %region_1.2_spmd} | conditional | bytes 8 | solution.py:666
  17.3 37.4 %gradient_routed.1 = (f32[2304,128]{1,0:T(8,128)S(1)}, f32[48,64]{1,0:T(8,128)S(1)}, f32[48,64]{1,0:T(8,128)S(1)}) custom-call(s32[1,1024]{1,0:T(1,128)S(1)} %get-tuple-element.30.idx, f32[48,1024]{1,0:T(8,128)S(1)} %get-tuple-element.31.left, f32[48,1024]{1,0:T(8,128)S(1)} %get-tuple-element.32.right, f32[1,512,2304]{2,1,0:T(8,128)S(1)} %get-tuple-element.33.cores, ...), custom_call_target="tpu_custom_call" | custom-call | tf_op jit(solution)/shard_map/cond/branch_1_fun/gradient_routed/pallas_call | solution.py:666
  55.0 5.4 %finish.1 = f32[64,2304]{1,0:T(8,128)} custom-call(f32[2304,128]{1,0:T(8,128)S(1)} %get-tuple-element.44.turned, f32[48,64]{1,0:T(8,128)S(1)} %get-tuple-element.45.hprev, f32[48,64]{1,0:T(8,128)S(1)} %get-tuple-element.46.hown), custom_call_target="tpu_custom_call" | custom-call | tf_op jit(solution)/shard_map/finish/pallas_call | solution.py:668
Async XLA Ops:
  0.7 0.7 %copy-start = (s32[1024,4]{0,1:T(4,128)S(1)}, s32[1024,4]{0,1:T(4,128)}, u32[]{:S(2)}) copy-start(s32[1024,4]{0,1:T(4,128)} %param.7) | copy-start | bytes 49156
  1.4 0.7 %copy-start.1 = (f32[1024]{0:T(1024)S(1)}, f32[1024]{0:T(1024)}, u32[]{:S(2)}) copy-start(f32[1024]{0:T(1024)} %param.8) | copy-start | bytes 12292
  2.1 15.2 %copy-start.2 = (f32[1,512,2304]{2,1,0:T(8,128)S(1)}, f32[1,512,2304]{2,1,0:T(8,128)}, u32[]{:S(2)}) copy-start(f32[1,512,2304]{2,1,0:T(8,128)} %cores.1) | copy-start | bytes 14155780

commit v5 on v4

--- a/solution.py
+++ b/solution.py
@@ -105,9 +105,8 @@
         lay(moved, weigh(hprev[...], ustack), slab)
         yh, yl = split(across(moved, slab))
         nt = (((1,), (1,)), ((), ()))
-        gram = lax.dot_general(zh, yh, nt, preferred_element_type=F32)
-        gram = gram + lax.dot_general(zh, yl, nt, preferred_element_type=F32)
-        gram = gram + lax.dot_general(zl, yh, nt, preferred_element_type=F32)
+        gram = lax.dot_general(jnp.concatenate([zh, zl], axis=0), yh, nt, preferred_element_type=F32)
+        gram = gram[:R] + gram[R:] + lax.dot_general(zh, yl, nt, preferred_element_type=F32)
         gram = jnp.concatenate([gram * (1.0 / N), jnp.zeros((R, W - R), F32)], axis=1)
         sendbuf[...] = jnp.concatenate([gram[:R // 2], gram[R // 2:]], axis=1)
         for d in range(nsamp):
@@ -183,9 +182,8 @@
     unit = (lax.broadcasted_iota(jnp.int32, (R, count), 0) == 0).astype(F32)
 
     def picked(part):
-        high, low = split(part.T)
-        return (jnp.dot(high, onehot, preferred_element_type=F32)
-                + jnp.dot(low, onehot, preferred_element_type=F32))
+        out = jnp.dot(jnp.concatenate(split(part.T), axis=0), onehot, preferred_element_type=F32)
+        return out[:part.shape[1]] + out[part.shape[1]:]
 
     @pl.when(first)
     def _():
@@ -529,11 +527,9 @@
             slices = jnp.where(lax.broadcasted_iota(jnp.int32, (slab, count), 0) == ids, 1.0, 0.0).astype(BF16)
             for t in range(0, R, 16):
                 outer = jnp.concatenate([vecs[a:a + 1] * vecs[R:2 * R] for a in range(t, t + 16)], axis=0)
-                high, low = split(outer)
+                out = lax.dot_general(jnp.concatenate(split(outer), axis=0), slices, nt, preferred_element_type=F32)
                 here = slice(t * R, t * R + step)
-                turned[here, 0:slab] = turned[here, 0:slab] - rate[0, 0] * (
-                    lax.dot_general(high, slices, nt, preferred_element_type=F32)
-                    + lax.dot_general(low, slices, nt, preferred_element_type=F32))
+                turned[here, 0:slab] = turned[here, 0:slab] - rate[0, 0] * (out[:step] + out[step:])
         for d in range(1, nsamp):
             send(d).wait_send()
 

time: 60.7 us -> 60.2 us (level)
  no operation moved by 1% of the time
where the time goes in v5:
time: 60.2 us; the launch traced here: 59.8 us
  Pallas kernels  56.2 us (93%)
  local copies, waits for them, and re-layouts  2.64 us (4%)
  between operations  0.68 us (1%)
    pallas_call x1, Pallas kernels, on_device(): lax.cond(over[0, 0] == 0.0, routed, summed, own_index.reshape(1, count),...  36.8 us
    pallas_call x1, Pallas kernels, on_device(): pl.pallas_call(functools.partial(front_kernel, ncores, nsamp, room), out_...  14 us
    pallas_call x1, Pallas kernels, on_device(): pl.pallas_call(finish_kernel, out_shape=new_slices, in_specs=[vm] * 3, ou...  5.4 us
    unnamed x6, local copies, waits for them, and re-layouts  1.41 us

profile of v5, /device:TPU:4, one launch (start us, length us, event | category | flops | bytes accessed | tf_op | source)
XLA Modules:
  0.0 59.8 jit_solution(5637217437812461132)
XLA Ops:
  0.0 0.7 %dynamic-slice_bitcast_fusion.idx = s32[1,1024]{1,0:T(1,128)S(1)} fusion(s32[1024,4]{0,1:T(4,128)} %param.7, s32[]{:T(128)S(6)} %select_n.4), kind=kLoop, calls=%fused_computation | loop fusion | bytes 8196 | tf_op jit(solution)/shard_map/reshape | solution.py:607
  0.7 0.0 copy-start
  0.7 0.7 %copy-done = s32[1024,4]{0,1:T(4,128)S(1)} copy-done((s32[1024,4]{0,1:T(4,128)S(1)}, s32[1024,4]{0,1:T(4,128)}, u32[]{:S(2)}) %copy-start) | copy-done | bytes 16408
  1.4 0.0 copy-start.1
  1.4 0.7 %copy-done.1 = f32[1024]{0:T(1024)S(1)} copy-done((f32[1024]{0:T(1024)S(1)}, f32[1024]{0:T(1024)}, u32[]{:S(2)}) %copy-start.1) | copy-done | bytes 4120
  2.1 0.0 copy-start.2
  2.1 14.0 %sample_vectors.1 = (f32[48,1024]{1,0:T(8,128)S(1)}, f32[48,1024]{1,0:T(8,128)S(1)}, f32[8,128]{1,0:T(8,128)S(1)}) custom-call(f32[1,512,2304]{2,1,0:T(8,128)} %cores.1, s32[1,1024]{1,0:T(1,128)S(1)} %dynamic-slice_bitcast_fusion.idx, s32[4,1024]{1,0:T(4,128)S(1)} %bitcast.7, f32[1,1024]{1,0:T(1,128)S(1)} %bitcast.8), custom_call_target="tpu_custom_call" | custom-call | tf_op jit(solution)/shard_map/sample_vectors/pallas_call | solution.py:585
  16.1 0.5 slice.3
  17.3 0.0 copy-done.2
  17.3 37.1 %conditional.1 = ((f32[2304,128]{1,0:T(8,128)S(1)}, f32[48,64]{1,0:T(8,128)S(1)}, f32[48,64]{1,0:T(8,128)S(1)})) conditional(s32[]{:T(128)} %bitcast.3, (s32[1,1024]{1,0:T(1,128)S(1)}, f32[48,1024]{1,0:T(8,128)S(1)}, f32[48,1024]{1,0:T(8,128)S(1)}, f32[1,512,2304]{2,1,0:T(8,128)S(1)}, f32[1,1]{1,0:T(1,128)}) %tuple.16, (s32[1,1024]{1,0:T(1,128)S(1)}, ...), branch_computations={%region_0.1_spmd, %region_1.2_spmd} | conditional | bytes 8 | solution.py:662
  17.3 36.8 %gradient_routed.1 = (f32[2304,128]{1,0:T(8,128)S(1)}, f32[48,64]{1,0:T(8,128)S(1)}, f32[48,64]{1,0:T(8,128)S(1)}) custom-call(s32[1,1024]{1,0:T(1,128)S(1)} %get-tuple-element.30.idx, f32[48,1024]{1,0:T(8,128)S(1)} %get-tuple-element.31.left, f32[48,1024]{1,0:T(8,128)S(1)} %get-tuple-element.32.right, f32[1,512,2304]{2,1,0:T(8,128)S(1)} %get-tuple-element.33.cores, ...), custom_call_target="tpu_custom_call" | custom-call | tf_op jit(solution)/shard_map/cond/branch_1_fun/gradient_routed/pallas_call | solution.py:662
  54.4 5.4 %finish.1 = f32[64,2304]{1,0:T(8,128)} custom-call(f32[2304,128]{1,0:T(8,128)S(1)} %get-tuple-element.44.turned, f32[48,64]{1,0:T(8,128)S(1)} %get-tuple-element.45.hprev, f32[48,64]{1,0:T(8,128)S(1)} %get-tuple-element.46.hown), custom_call_target="tpu_custom_call" | custom-call | tf_op jit(solution)/shard_map/finish/pallas_call | solution.py:664
Async XLA Ops:
  0.7 0.7 %copy-start = (s32[1024,4]{0,1:T(4,128)S(1)}, s32[1024,4]{0,1:T(4,128)}, u32[]{:S(2)}) copy-start(s32[1024,4]{0,1:T(4,128)} %param.7) | copy-start | bytes 49156
  1.4 0.7 %copy-start.1 = (f32[1024]{0:T(1024)S(1)}, f32[1024]{0:T(1024)}, u32[]{:S(2)}) copy-start(f32[1024]{0:T(1024)} %param.8) | copy-start | bytes 12292
  2.1 15.2 %copy-start.2 = (f32[1,512,2304]{2,1,0:T(8,128)S(1)}, f32[1,512,2304]{2,1,0:T(8,128)}, u32[]{:S(2)}) copy-start(f32[1,512,2304]{2,1,0:T(8,128)} %cores.1) | copy-start | bytes 14155780
